TPU v7x, 32 devices: a whole 2x2x4 slice. The times are simulated.
32 devices in a mesh: sweep: 2 (over y), dp: 8 (over z, x), mp: 2 (over core).
Axes of the slice: x: 2, y: 2, z: 4, core: 2. Of those that a mesh axis runs over, the one named last changes fastest.
Arguments:
- tokens: bfloat16 [128, 6144], P(('sweep', 'dp'), 'mp'), parts along dimension 0, may hold values from -6 to 6
- cotangent: bfloat16 [128, 6144], P(('sweep', 'dp'), 'mp'), parts along dimension 0, may hold values from -6 to 6
- inward_blocks: bfloat16 [4, 8, 576, 128, 128], P(('sweep', 'mp'), 'dp'), parts along dimension 0, may hold values from -0.109375 to 0.109375
- inward_rows: int32 [4, 8, 576], P(('sweep', 'mp'), 'dp'), parts along dimension 0, may hold values from 0 to 23, as said below
- inward_cols: int32 [4, 8, 576], P(('sweep', 'mp'), 'dp'), parts along dimension 0, may hold values from 0 to 23
- inward_count: int32 [4, 8], P(('sweep', 'mp'), 'dp'), parts along dimension 0, may hold values from 72 to 576, as said below
- outward_blocks: bfloat16 [16, 2, 576, 128, 128], P(('sweep', 'dp'), 'mp'), parts along dimension 0, may hold values from -0.0546875 to 0.0546875
- outward_rows: int32 [16, 2, 576], P(('sweep', 'dp'), 'mp'), parts along dimension 0, may hold values from 0 to 23, as said below
- outward_cols: int32 [16, 2, 576], P(('sweep', 'dp'), 'mp'), parts along dimension 0, may hold values from 0 to 23
- outward_count: int32 [16, 2], P(('sweep', 'dp'), 'mp'), parts along dimension 0, may hold values from 72 to 576, as said below
Outputs:
- out_tokens: bfloat16 [128, 6144], P(('sweep', 'dp'), 'mp'), parts along dimension 0
- grad_tokens: bfloat16 [128, 6144], P(('sweep', 'dp'), 'mp'), parts along dimension 0
- grad_inward: bfloat16 [4, 8, 576, 128, 128], P(('sweep', 'mp'), 'dp'), parts along dimension 0
- grad_outward: bfloat16 [16, 2, 576, 128, 128], P(('sweep', 'dp'), 'mp'), parts along dimension 0
There are 2 independent parts, one for each index of `sweep`. A program takes and returns all parts, laid end to end along the dimension named above; each array names one. Nothing has to cross between parts.
Inputs may be any that keep to these rules, and one draw needn't show every extreme that they name: In every shard, inward_rows and inward_cols together name each of the 24 x 24 block positions of its region exactly once; the first inward_count slots hold the kept blocks, the others are padding. `inward_count`: some shard keeps all 576 blocks in every draw. In every shard, outward_rows and outward_cols together name each of the 24 x 24 block positions of its region exactly once; the first outward_count slots hold the kept blocks, the others are padding. `outward_count`: some shard keeps all 576 blocks in every draw.
All inputs are finite; a program needn't handle non-finite values.
Results may differ from a plain program's by a relative error of at most 0.0051.
Values may be sent and summed in bfloat16 or wider, within the bound.
No kernel may reach another device: no remote copies, remote signals or barrier semaphores. Data moves between devices by JAX's collectives and lax.ppermute only.
A program may use at most 256 MiB of HBM per device.

v0:
```python
import functools

import jax
import jax.numpy as jnp
from jax import lax
from jax.experimental import pallas as pl
from jax.experimental.pallas import tpu as pltpu
from jax.sharding import PartitionSpec as P

root_half = 0.7071067811865476
inv_root_tau = 0.3989422804014327

SMEM = pl.BlockSpec(memory_space=pltpu.SMEM)
VMEM = pl.BlockSpec(memory_space=pltpu.VMEM)
ANY = pl.BlockSpec(memory_space=pl.ANY)
MIB = 1 << 20


def gelu_curve(values):
    return 0.5 * values * (1.0 + lax.erf(values * root_half))


def gelu_slope(values):
    return (
        0.5 * (1.0 + lax.erf(values * root_half))
        + values * jnp.exp(-0.5 * values * values) * inv_root_tau
    )


def slots_kernel(row_blocks, col_blocks, in_rows, in_cols, out_rows, out_cols, in_slots, out_slots):
    def place(slot, carry):
        in_slots[in_rows[slot] * col_blocks + in_cols[slot]] = slot
        out_slots[out_rows[slot] * row_blocks + out_cols[slot]] = slot
        return carry

    lax.fori_loop(0, in_rows.shape[0], place, 0, unroll=8)


def slot_maps(in_rows, in_cols, out_rows, out_cols, row_blocks, col_blocks):
    shape = jax.ShapeDtypeStruct(in_rows.shape, jnp.int32)
    return pl.pallas_call(
        functools.partial(slots_kernel, row_blocks, col_blocks),
        out_shape=(shape, shape),
        in_specs=[SMEM] * 4,
        out_specs=(SMEM, SMEM),
        name="slot_maps",
    )(in_rows, in_cols, out_rows, out_cols)


def pair(count):
    return 2 if count % 2 == 0 else 1


def multiply(lhs_ref, blocks_ref, slots_ref, kept, depth, width, across, store):
    side = blocks_ref.shape[-1]
    deep, wide = pair(depth), pair(width)

    def block(k, n):
        position = n * depth + k if across else k * width + n
        slot = slots_ref[position]
        found = blocks_ref[slot]
        return jnp.where(slot < kept, found, jnp.zeros_like(found))

    def column(step, carry):
        n0 = step * wide
        total = None
        for k0 in range(0, depth, deep):
            if across:
                tile = jnp.concatenate(
                    [
                        jnp.concatenate([block(k0 + k, n0 + n) for k in range(deep)], axis=1)
                        for n in range(wide)
                    ],
                    axis=0,
                )
                dims = (((1,), (1,)), ((), ()))
            else:
                tile = jnp.concatenate(
                    [
                        jnp.concatenate([block(k0 + k, n0 + n) for n in range(wide)], axis=1)
                        for k in range(deep)
                    ],
                    axis=0,
                )
                dims = (((1,), (0,)), ((), ()))
            lhs = lhs_ref[:, k0 * side : (k0 + deep) * side]
            part = lax.dot_general(lhs, tile, dims, preferred_element_type=jnp.float32)
            total = part if total is None else total + part
        store(pl.multiple_of(n0 * side, wide * side), wide * side, total)
        return carry

    lax.fori_loop(0, width // wide, column, 0)


def first_kernel(depth, width, across, slots, kept, lhs, blocks, own, sent):
    def store(start, size, total):
        own[:, pl.ds(start, size)] = total
        sent[:, pl.ds(start, size)] = total.astype(jnp.bfloat16)

    multiply(lhs, blocks, slots, kept[0], depth, width, across, store)


def first_product(slots, kept, lhs, blocks, depth, width, across, name):
    shape = (lhs.shape[0], width * blocks.shape[-1])
    return pl.pallas_call(
        functools.partial(first_kernel, depth, width, across),
        out_shape=(jax.ShapeDtypeStruct(shape, jnp.float32), jax.ShapeDtypeStruct(shape, jnp.bfloat16)),
        in_specs=[SMEM, SMEM, VMEM, VMEM],
        out_specs=(VMEM, VMEM),
        compiler_params=pltpu.CompilerParams(vmem_limit_bytes=8 * MIB),
        cost_estimate=pl.CostEstimate(
            flops=2 * lhs.size * width * blocks.shape[-1], bytes_accessed=4 * MIB, transcendentals=0
        ),
        name=name,
    )(slots, kept, lhs, in_vmem(blocks))


def in_vmem(blocks):
    return pltpu.with_memory_space_constraint(blocks, pltpu.VMEM)


def spread(parts, rows):
    def store(start, size, total):
        rounded = total.astype(jnp.bfloat16)
        for index, part in enumerate(parts):
            part[:, pl.ds(start, size)] = rounded[index * rows : (index + 1) * rows]

    return store


def output_kernel(depth, width, rows, slots, kept, own, other, blocks, activated, *parts):
    side = blocks.shape[-1]

    def activate(step, carry):
        at = pl.ds(pl.multiple_of(step * side, side), side)
        hidden = own[:, at] + other[:, at].astype(jnp.float32)
        activated[:, at] = gelu_curve(hidden).astype(jnp.bfloat16)
        return carry

    lax.fori_loop(0, depth, activate, 0)
    multiply(activated, blocks, slots, kept[0], depth, width, False, spread(parts, rows))


def gradient_kernel(
    depth, width, rows, slots, kept, hid_own, hid_other, act_own, act_other, blocks, grad_hidden, *parts
):
    side = blocks.shape[-1]

    def activate(step, carry):
        at = pl.ds(pl.multiple_of(step * side, side), side)
        hidden = hid_own[:, at] + hid_other[:, at].astype(jnp.float32)
        grad_act = act_own[:, at] + act_other[:, at].astype(jnp.float32)
        grad_hidden[:, at] = (grad_act * gelu_slope(hidden)).astype(jnp.bfloat16)
        return carry

    lax.fori_loop(0, depth, activate, 0)
    multiply(grad_hidden, blocks, slots, kept[0], depth, width, True, spread(parts, rows))


def second_product(body, slots, kept, values, blocks, depth, width, pieces, name):
    count = values[0].shape[0]
    side = blocks.shape[-1]
    rows = count // pieces
    shapes = [jax.ShapeDtypeStruct((count, depth * side), jnp.bfloat16)]
    shapes += [jax.ShapeDtypeStruct((rows, width * side), jnp.bfloat16)] * pieces
    middle, *parts = pl.pallas_call(
        functools.partial(body, depth, width, rows),
        out_shape=tuple(shapes),
        in_specs=[SMEM, SMEM] + [VMEM] * (len(values) + 1),
        out_specs=(VMEM,) * len(shapes),
        compiler_params=pltpu.CompilerParams(vmem_limit_bytes=10 * MIB),
        cost_estimate=pl.CostEstimate(
            flops=2 * count * depth * width * side * side, bytes_accessed=6 * MIB, transcendentals=0
        ),
        name=name,
    )(slots, kept, *values, in_vmem(blocks))
    return middle, parts


def outer_kernel(tall, wide, slots, kept_ref, left, right, result, turned, stage, sems):
    count = left.shape[0]
    side = result.shape[-1]
    step_width = pair(wide)
    steps = wide // step_width
    buffers = stage.shape[0]
    kept = kept_ref[0]
    scale = float(count) ** (-0.5)
    zero_at = tall * step_width

    for a in range(tall):
        turned[a] = left[:, a * side : (a + 1) * side].T
    for buffer in range(buffers):
        stage[buffer, zero_at] = jnp.zeros((side, side), jnp.bfloat16)

    def wait(buffer):
        pltpu.make_async_copy(
            stage.at[buffer, pl.ds(0, zero_at)], result.at[pl.ds(0, zero_at)], sems.at[buffer]
        ).wait()

    def step(index, carry):
        buffer = lax.rem(index, buffers)

        @pl.when(index >= buffers)
        def _():
            wait(buffer)

        at = pl.ds(pl.multiple_of(index * step_width * side, step_width * side), step_width * side)
        values = right[:, at]
        for a in range(tall):
            tile = jnp.dot(turned[a], values, preferred_element_type=jnp.float32) * scale
            tile = tile.astype(jnp.bfloat16)
            for b in range(step_width):
                stage[buffer, a * step_width + b] = tile[:, b * side : (b + 1) * side]
                slot = slots[a * wide + index * step_width + b]
                source = jnp.where(slot < kept, a * step_width + b, zero_at)
                pltpu.make_async_copy(
                    stage.at[buffer, source], result.at[slot], sems.at[buffer]
                ).start()
        return carry

    lax.fori_loop(0, steps, step, 0)
    for index in range(max(0, steps - buffers), steps):
        wait(index % buffers)


def outer_product(slots, kept, left, right, side, name):
    count = left.shape[0]
    tall, wide = left.shape[1] // side, right.shape[1] // side
    buffers = min(3, wide // pair(wide))
    return pl.pallas_call(
        functools.partial(outer_kernel, tall, wide),
        out_shape=jax.ShapeDtypeStruct((tall * wide, side, side), jnp.bfloat16),
        in_specs=[SMEM, SMEM, VMEM, VMEM],
        out_specs=ANY,
        scratch_shapes=[
            pltpu.VMEM((tall, side, count), jnp.bfloat16),
            pltpu.VMEM((buffers, tall * pair(wide) + 1, side, side), jnp.bfloat16),
            pltpu.SemaphoreType.DMA((buffers,)),
        ],
        compiler_params=pltpu.CompilerParams(vmem_limit_bytes=14 * MIB),
        cost_estimate=pl.CostEstimate(
            flops=8 * left.size * right.shape[1],
            bytes_accessed=2 * tall * wide * side * side,
            transcendentals=0,
        ),
        name=name,
    )(slots, kept, left, right)


def gather(values, devices):
    if devices > 8:
        return lax.all_gather(values, "dp", axis=0, tiled=True)
    pieces = [values]
    for away in range(1, devices):
        path = [(i, (i + away) % devices) for i in range(devices)]
        pieces.append(lax.ppermute(values, "dp", path))
    return jnp.concatenate(pieces, axis=0)


def scatter(parts, devices):
    if devices > 8:
        whole = jnp.concatenate(parts, axis=0).astype(jnp.float32)
        return lax.psum_scatter(whole, "dp", scatter_dimension=0, tiled=True).astype(jnp.bfloat16)
    total = parts[0].astype(jnp.float32)
    for away in range(1, devices):
        path = [(i, (i - away) % devices) for i in range(devices)]
        total = total + lax.ppermute(parts[away], "dp", path).astype(jnp.float32)
    return total.astype(jnp.bfloat16)


def swap(values, devices):
    return lax.ppermute(values, "mp", [(i, (i + 1) % devices) for i in range(devices)])


def shards(
    tokens,
    cotangent,
    inward_blocks,
    inward_rows,
    inward_cols,
    inward_count,
    outward_blocks,
    outward_rows,
    outward_cols,
    outward_count,
):
    side = inward_blocks.shape[-1]
    region = inward_blocks.shape[2]
    row_blocks = tokens.shape[1] // side
    col_blocks = region // row_blocks
    n_dp = lax.axis_size("dp")
    n_mp = lax.axis_size("mp")
    in_kept = inward_count.reshape(1)
    out_kept = outward_count.reshape(1)
    inward = inward_blocks.reshape(region, side, side)
    outward = outward_blocks.reshape(region, side, side)
    in_slots, out_slots = slot_maps(
        inward_rows.reshape(region),
        inward_cols.reshape(region),
        outward_rows.reshape(region),
        outward_cols.reshape(region),
        row_blocks,
        col_blocks,
    )
    all_tokens = gather(tokens, n_dp)
    all_grads = gather(cotangent, n_dp)
    hid_own, hid_sent = first_product(
        in_slots, in_kept, all_tokens, inward, row_blocks, col_blocks, False, "hidden"
    )
    hid_other = swap(hid_sent, n_mp)
    act_own, act_sent = first_product(
        out_slots, out_kept, all_grads, outward, row_blocks, col_blocks, True, "grad_act"
    )
    act_other = swap(act_sent, n_mp)
    activated, out_parts = second_product(
        output_kernel, out_slots, out_kept, (hid_own, hid_other), outward, col_blocks, row_blocks, n_dp, "output"
    )
    out_tokens = scatter(out_parts, n_dp)
    grad_hidden, in_parts = second_product(
        gradient_kernel,
        in_slots,
        in_kept,
        (hid_own, hid_other, act_own, act_other),
        inward,
        col_blocks,
        row_blocks,
        n_dp,
        "grad_tokens",
    )
    grad_tokens = scatter(in_parts, n_dp)
    grad_outward = outer_product(out_slots, out_kept, activated, all_grads, side, "outward")
    grad_inward = outer_product(in_slots, in_kept, all_tokens, grad_hidden, side, "inward")
    return (
        out_tokens,
        grad_tokens,
        grad_inward.reshape(inward_blocks.shape),
        grad_outward.reshape(outward_blocks.shape),
    )


def solution(mesh):
    in_specs = (
        P(("sweep", "dp"), "mp"),
        P(("sweep", "dp"), "mp"),
        P(("sweep", "mp"), "dp", None, None, None),
        P(("sweep", "mp"), "dp", None),
        P(("sweep", "mp"), "dp", None),
        P(("sweep", "mp"), "dp"),
        P(("sweep", "dp"), "mp", None, None, None),
        P(("sweep", "dp"), "mp", None),
        P(("sweep", "dp"), "mp", None),
        P(("sweep", "dp"), "mp"),
    )
    out_specs = (
        P(("sweep", "dp"), "mp"),
        P(("sweep", "dp"), "mp"),
        P(("sweep", "mp"), "dp", None, None, None),
        P(("sweep", "dp"), "mp", None, None, None),
    )
    return jax.shard_map(shards, mesh=mesh, in_specs=in_specs, out_specs=out_specs, check_vma=False)
```

profile of v0, /device:TPU:0, one launch (start us, length us, event | category | flops | bytes accessed | tf_op | source)
XLA Modules:
  0.0 153.0 jit_solution(17775927743871235172)
XLA Ops:
  0.6 5.1 %collective-permute-start.5 = (bf16[8,3072]{1,0:T(8,128)(2,1)}, bf16[8,3072]{1,0:T(8,128)(2,1)S(1)}, u32[]{:S(2)}, u32[]{:S(2)}) collective-permute-start(bf16[8,3072]{1,0:T(8,128)(2,1)} %param.10), channel_id=1, source_target_pairs={{0,12},{2,14},{4,0},{6,2},{8,4},{10,6},{12,8},{14,10},{1,13},{3,15... | collective-permute-start | bytes 147464 | tf_op jit(solution)/shard_map/ppermute | solution.py:256
  6.1 3.5 %collective-permute-start.3 = (bf16[8,3072]{1,0:T(8,128)(2,1)}, bf16[8,3072]{1,0:T(8,128)(2,1)S(1)}, u32[]{:S(2)}, u32[]{:S(2)}) collective-permute-start(bf16[8,3072]{1,0:T(8,128)(2,1)} %param.10), channel_id=1, source_target_pairs={{0,8},{2,10},{4,12},{6,14},{8,0},{10,2},{12,4},{14,6},{1,9},{3,11}... | collective-permute-start | bytes 147464 | tf_op jit(solution)/shard_map/ppermute | solution.py:256
  9.6 1.5 collective-permute-start
  14.0 1.3 reduce.in_rows
  19.1 3.8 %slot_maps.1 = (s32[576]{0:T(1024)}, s32[576]{0:T(1024)}) custom-call(s32[576]{0:T(1024)} %reduce.in_rows, s32[576]{0:T(1024)} %reduce.1.in_cols, s32[576]{0:T(1024)} %reduce.2.out_rows, s32[576]{0:T(1024)} %reduce.3.out_cols), custom_call_target="tpu_custom_call" | custom-call | tf_op jit(solution)/shard_map/slot_maps/pallas_call | solution.py:41
  24.1 5.1 %collective-permute-done.1 = bf16[8,3072]{1,0:T(8,128)(2,1)S(1)} collective-permute-done((bf16[8,3072]{1,0:T(8,128)(2,1)}, bf16[8,3072]{1,0:T(8,128)(2,1)S(1)}, u32[]{:S(2)}, u32[]{:S(2)}) %collective-permute-start.1) | collective-permute-done | bytes 49184 | tf_op jit(solution)/shard_map/ppermute | solution.py:256
  30.1 6.0 %collective-permute-done.15 = bf16[8,3072]{1,0:T(8,128)(2,1)S(1)} collective-permute-done((bf16[8,3072]{1,0:T(8,128)(2,1)}, bf16[8,3072]{1,0:T(8,128)(2,1)S(1)}, u32[]{:S(2)}, u32[]{:S(2)}) %collective-permute-start.15) | collective-permute-done | bytes 49184 | tf_op jit(solution)/shard_map/ppermute | solution.py:256
  36.2 6.1 %collective-permute-done.16 = bf16[8,3072]{1,0:T(8,128)(2,1)S(1)} collective-permute-done((bf16[8,3072]{1,0:T(8,128)(2,1)}, bf16[8,3072]{1,0:T(8,128)(2,1)S(1)}, u32[]{:S(2)}, u32[]{:S(2)}) %collective-permute-start.16) | collective-permute-done | bytes 49184 | tf_op jit(solution)/shard_map/ppermute | solution.py:256
  42.3 6.3 %collective-permute-done.17 = bf16[8,3072]{1,0:T(8,128)(2,1)S(1)} collective-permute-done((bf16[8,3072]{1,0:T(8,128)(2,1)}, bf16[8,3072]{1,0:T(8,128)(2,1)S(1)}, u32[]{:S(2)}, u32[]{:S(2)}) %collective-permute-start.17) | collective-permute-done | bytes 49184 | tf_op jit(solution)/shard_map/ppermute | solution.py:256
  48.6 5.2 %collective-permute-done.18 = bf16[8,3072]{1,0:T(8,128)(2,1)S(1)} collective-permute-done((bf16[8,3072]{1,0:T(8,128)(2,1)}, bf16[8,3072]{1,0:T(8,128)(2,1)S(1)}, u32[]{:S(2)}, u32[]{:S(2)}) %collective-permute-start.18) | collective-permute-done | bytes 49184 | tf_op jit(solution)/shard_map/ppermute | solution.py:256
  53.8 5.2 %collective-permute-done.19 = bf16[8,3072]{1,0:T(8,128)(2,1)S(1)} collective-permute-done((bf16[8,3072]{1,0:T(8,128)(2,1)}, bf16[8,3072]{1,0:T(8,128)(2,1)S(1)}, u32[]{:S(2)}, u32[]{:S(2)}) %collective-permute-start.19) | collective-permute-done | bytes 49184 | tf_op jit(solution)/shard_map/ppermute | solution.py:256
  59.0 1.4 collective-permute-start.20
  60.4 2.9 %collective-permute-done.20 = bf16[8,3072]{1,0:T(8,128)(2,1)S(1)} collective-permute-done((bf16[8,3072]{1,0:T(8,128)(2,1)}, bf16[8,3072]{1,0:T(8,128)(2,1)S(1)}, u32[]{:S(2)}, u32[]{:S(2)}) %collective-permute-start.20) | collective-permute-done | bytes 49184 | tf_op jit(solution)/shard_map/ppermute | solution.py:256
  63.3 1.7 %collective-permute-start.21 = (bf16[8,3072]{1,0:T(8,128)(2,1)}, bf16[8,3072]{1,0:T(8,128)(2,1)S(1)}, u32[]{:S(2)}, u32[]{:S(2)}) collective-permute-start(bf16[8,3072]{1,0:T(8,128)(2,1)} %param.11), channel_id=1, source_target_pairs={{0,14},{2,0},{4,2},{6,4},{8,6},{10,8},{12,10},{14,12},{1,15},{3,1}... | collective-permute-start | bytes 147464 | tf_op jit(solution)/shard_map/ppermute | solution.py:256
  65.0 2.6 %collective-permute-done.21 = bf16[8,3072]{1,0:T(8,128)(2,1)S(1)} collective-permute-done((bf16[8,3072]{1,0:T(8,128)(2,1)}, bf16[8,3072]{1,0:T(8,128)(2,1)S(1)}, u32[]{:S(2)}, u32[]{:S(2)}) %collective-permute-start.21) | collective-permute-done | bytes 49184 | tf_op jit(solution)/shard_map/ppermute | solution.py:256
  67.6 4.4 %collective-permute-start.6 = (bf16[8,3072]{1,0:T(8,128)(2,1)}, bf16[8,3072]{1,0:T(8,128)(2,1)S(1)}, u32[]{:S(2)}, u32[]{:S(2)}) collective-permute-start(bf16[8,3072]{1,0:T(8,128)(2,1)} %param.10), channel_id=1, source_target_pairs={{0,14},{2,0},{4,2},{6,4},{8,6},{10,8},{12,10},{14,12},{1,15},{3,1}... | collective-permute-start | bytes 147464 | tf_op jit(solution)/shard_map/ppermute | solution.py:256
  72.0 6.4 %copy-done.1 = bf16[1,1,576,128,128]{4,3,2,1,0:T(8,128)(2,1)S(1)} copy-done((bf16[1,1,576,128,128]{4,3,2,1,0:T(8,128)(2,1)S(1)}, bf16[1,1,576,128,128]{4,3,2,1,0:T(8,128)(2,1)}, u32[]{:S(2)}) %copy-start.1) | copy-done | bytes 18874392
  79.0 8.0 %grad_act.1 = (f32[64,3072]{1,0:T(8,128)S(1)}, bf16[64,3072]{1,0:T(8,128)(2,1)S(1)}) custom-call(s32[576]{0:T(1024)S(1)} %copy-done.2, s32[1]{0:T(128)} %bitcast.10.kept, bf16[64,3072]{1,0:T(8,128)(2,1)S(1)} %constant_dynamic-update-slice_fusion.8.lhs.right, bf16[576,128,128]{2,1,0:T(8,128)(2,1)S(1)} %bitcast.14), custom_call_target="tpu_custom_call" | custom-call | flops 1207959552 | bytes 4194304 | tf_op jit(solution)/shard_map/grad_act/pallas_call | solution.py:105
  87.2 5.9 %hidden.1 = (f32[64,3072]{1,0:T(8,128)S(1)}, bf16[64,3072]{1,0:T(8,128)(2,1)S(1)}) custom-call(s32[576]{0:T(1024)S(1)} %copy-done.4, s32[1]{0:T(128)} %bitcast.6.kept, bf16[64,3072]{1,0:T(8,128)(2,1)S(1)} %constant_dynamic-update-slice_fusion.lhs.left, bf16[576,128,128]{2,1,0:T(8,128)(2,1)S(1)} %bitcast.12), custom_call_target="tpu_custom_call" | custom-call | flops 1207959552 | bytes 4194304 | tf_op jit(solution)/shard_map/hidden/pallas_call | solution.py:105
  93.7 1.3 collective-permute-done.7.other.hid_other
  95.0 8.6 %grad_tokens.1 = (bf16[64,3072]{1,0:T(8,128)(2,1)S(1)}, bf16[8,3072]{1,0:T(8,128)(2,1)S(1)}, bf16[8,3072]{1,0:T(8,128)(2,1)S(1)}, bf16[8,3072]{1,0:T(8,128)(2,1)...) custom-call(s32[576]{0:T(1024)S(1)} %copy-done.4, ...), custom_call_target="tpu_custom_call" | custom-call | flops 1207959552 | bytes 6291456 | tf_op jit(solution)/shard_map/grad_tokens/pallas_call | solution.py:166
  105.0 3.3 %collective-permute-start.26 = (bf16[8,3072]{1,0:T(8,128)(2,1)S(1)}, bf16[8,3072]{1,0:T(8,128)(2,1)S(1)}, u32[]{:S(2)}, u32[]{:S(2)}) collective-permute-start(bf16[8,3072]{1,0:T(8,128)(2,1)S(1)} %get-tuple-element.46), channel_id=1, source_target_pairs={{0,8},{2,10},{4,12},{6,14},{8,0},{10,2},{12,4},{14,6},{1,9},{3,11}... | collective-permute-start | bytes 147464 | tf_op jit(solution)/shard_map/ppermute | solution.py:267
  108.3 8.5 %inward.1 = bf16[576,128,128]{2,1,0:T(8,128)(2,1)} custom-call(s32[576]{0:T(1024)S(1)} %copy-done.4, s32[1]{0:T(128)} %bitcast.8.kept_ref, bf16[64,3072]{1,0:T(8,128)(2,1)S(1)} %constant_dynamic-update-slice_fusion.lhs.left, bf16[64,3072]{1,0:T(8,128)(2,1)S(1)} %get-tuple-element.50.right), custom_call_target="tpu_custom_call" | custom-call | flops 4831838208 | bytes 18874368 | tf_op jit(solution)/shard_map/inward/pallas_call | solution.py:230
  116.9 6.4 %output.1 = (bf16[64,3072]{1,0:T(8,128)(2,1)S(1)}, bf16[8,3072]{1,0:T(8,128)(2,1)S(1)}, bf16[8,3072]{1,0:T(8,128)(2,1)S(1)}, bf16[8,3072]{1,0:T(8,128)(2,1)S(1)}...) custom-call(s32[576]{0:T(1024)S(1)} %copy-done.3, ...), custom_call_target="tpu_custom_call" | custom-call | flops 1207959552 | bytes 6291456 | tf_op jit(solution)/shard_map/output/pallas_call | solution.py:166
  123.3 1.9 %collective-permute-start.28 = (bf16[8,3072]{1,0:T(8,128)(2,1)S(1)}, bf16[8,3072]{1,0:T(8,128)(2,1)S(1)}, u32[]{:S(2)}, u32[]{:S(2)}) collective-permute-start(bf16[8,3072]{1,0:T(8,128)(2,1)S(1)} %get-tuple-element.48), channel_id=1, source_target_pairs={{0,4},{2,6},{4,8},{6,10},{8,12},{10,14},{12,0},{14,2},{1,5},{3,7},... | collective-permute-start | bytes 147464 | tf_op jit(solution)/shard_map/ppermute | solution.py:267
  125.2 1.5 collective-permute-start.29
  126.6 3.3 %collective-permute-start.8 = (bf16[8,3072]{1,0:T(8,128)(2,1)S(1)}, bf16[8,3072]{1,0:T(8,128)(2,1)S(1)}, u32[]{:S(2)}, u32[]{:S(2)}) collective-permute-start(bf16[8,3072]{1,0:T(8,128)(2,1)S(1)} %get-tuple-element.33), channel_id=1, source_target_pairs={{0,14},{2,0},{4,2},{6,4},{8,6},{10,8},{12,10},{14,12},{1,15},{3,1}... | collective-permute-start | bytes 147464 | tf_op jit(solution)/shard_map/ppermute | solution.py:267
  130.8 8.3 %outward.1 = bf16[576,128,128]{2,1,0:T(8,128)(2,1)} custom-call(s32[576]{0:T(1024)S(1)} %copy-done.3, s32[1]{0:T(128)} %bitcast.11.kept_ref, bf16[64,3072]{1,0:T(8,128)(2,1)S(1)} %get-tuple-element.51.left, bf16[64,3072]{1,0:T(8,128)(2,1)S(1)} %constant_dynamic-update-slice_fusion.8.lhs.right), custom_call_target="tpu_custom_call" | custom-call | flops 4831838208 | bytes 18874368 | tf_op jit(solution)/shard_map/outward/pallas_call | solution.py:230
  139.7 2.2 %collective-permute-start.11 = (bf16[8,3072]{1,0:T(8,128)(2,1)S(1)}, bf16[8,3072]{1,0:T(8,128)(2,1)S(1)}, u32[]{:S(2)}, u32[]{:S(2)}) collective-permute-start(bf16[8,3072]{1,0:T(8,128)(2,1)S(1)} %get-tuple-element.36), channel_id=1, source_target_pairs={{0,8},{2,10},{4,12},{6,14},{8,0},{10,2},{12,4},{14,6},{1,9},{3,11}... | collective-permute-start | bytes 147464 | tf_op jit(solution)/shard_map/ppermute | solution.py:267
  142.6 2.9 %collective-permute-start.13 = (bf16[8,3072]{1,0:T(8,128)(2,1)S(1)}, bf16[8,3072]{1,0:T(8,128)(2,1)S(1)}, u32[]{:S(2)}, u32[]{:S(2)}) collective-permute-start(bf16[8,3072]{1,0:T(8,128)(2,1)S(1)} %get-tuple-element.38), channel_id=1, source_target_pairs={{0,4},{2,6},{4,8},{6,10},{8,12},{10,14},{12,0},{14,2},{1,5},{3,7},... | collective-permute-start | bytes 147464 | tf_op jit(solution)/shard_map/ppermute | solution.py:267
  146.6 2.1 %collective-permute-done.12 = bf16[8,3072]{1,0:T(8,128)(2,1)S(1)} collective-permute-done((bf16[8,3072]{1,0:T(8,128)(2,1)S(1)}, bf16[8,3072]{1,0:T(8,128)(2,1)S(1)}, u32[]{:S(2)}, u32[]{:S(2)}) %collective-permute-start.12) | collective-permute-done | bytes 49184 | tf_op jit(solution)/shard_map/ppermute | solution.py:267
  149.1 3.2 %collective-permute-done.14 = bf16[8,3072]{1,0:T(8,128)(2,1)S(1)} collective-permute-done((bf16[8,3072]{1,0:T(8,128)(2,1)S(1)}, bf16[8,3072]{1,0:T(8,128)(2,1)S(1)}, u32[]{:S(2)}, u32[]{:S(2)}) %collective-permute-start.14) | collective-permute-done | bytes 49184 | tf_op jit(solution)/shard_map/ppermute | solution.py:267
  (78 shorter events, 15.1 us)
Async XLA Ops:
  0.6 86.5 %collective-permute-start.5 = (bf16[8,3072]{1,0:T(8,128)(2,1)}, bf16[8,3072]{1,0:T(8,128)(2,1)S(1)}, u32[]{:S(2)}, u32[]{:S(2)}) collective-permute-start(bf16[8,3072]{1,0:T(8,128)(2,1)} %param.10), channel_id=1, source_target_pairs={{0,12},{2,14},{4,0},{6,2},{8,4},{10,6},{12,8},{14,10},{1,13},{3,15... | collective-permute-start | bytes 147464 | tf_op jit(solution)/shard_map/ppermute | solution.py:256
  5.7 81.4 %collective-permute-start.4 = (bf16[8,3072]{1,0:T(8,128)(2,1)}, bf16[8,3072]{1,0:T(8,128)(2,1)S(1)}, u32[]{:S(2)}, u32[]{:S(2)}) collective-permute-start(bf16[8,3072]{1,0:T(8,128)(2,1)} %param.10), channel_id=1, source_target_pairs={{0,10},{2,12},{4,14},{6,0},{8,2},{10,4},{12,6},{14,8},{1,11},{3,13... | collective-permute-start | bytes 147464 | tf_op jit(solution)/shard_map/ppermute | solution.py:256
  6.1 81.0 %collective-permute-start.3 = (bf16[8,3072]{1,0:T(8,128)(2,1)}, bf16[8,3072]{1,0:T(8,128)(2,1)S(1)}, u32[]{:S(2)}, u32[]{:S(2)}) collective-permute-start(bf16[8,3072]{1,0:T(8,128)(2,1)} %param.10), channel_id=1, source_target_pairs={{0,8},{2,10},{4,12},{6,14},{8,0},{10,2},{12,4},{14,6},{1,9},{3,11}... | collective-permute-start | bytes 147464 | tf_op jit(solution)/shard_map/ppermute | solution.py:256
  9.6 77.4 %collective-permute-start.2 = (bf16[8,3072]{1,0:T(8,128)(2,1)}, bf16[8,3072]{1,0:T(8,128)(2,1)S(1)}, u32[]{:S(2)}, u32[]{:S(2)}) collective-permute-start(bf16[8,3072]{1,0:T(8,128)(2,1)} %param.10), channel_id=1, source_target_pairs={{0,6},{2,8},{4,10},{6,12},{8,14},{10,0},{12,2},{14,4},{1,7},{3,9},... | collective-permute-start | bytes 147464 | tf_op jit(solution)/shard_map/ppermute | solution.py:256
  9.6 13.4 %collective-permute-start = (bf16[8,3072]{1,0:T(8,128)(2,1)}, bf16[8,3072]{1,0:T(8,128)(2,1)S(1)}, u32[]{:S(2)}, u32[]{:S(2)}) collective-permute-start(bf16[8,3072]{1,0:T(8,128)(2,1)} %param.10), channel_id=1, source_target_pairs={{0,2},{2,4},{4,6},{6,8},{8,10},{10,12},{12,14},{14,0},{1,3},{3,5},... | collective-permute-start | bytes 147464 | tf_op jit(solution)/shard_map/ppermute | solution.py:256
  23.0 64.2 %copy-start = (bf16[1,1,576,128,128]{4,3,2,1,0:T(8,128)(2,1)S(1)}, bf16[1,1,576,128,128]{4,3,2,1,0:T(8,128)(2,1)}, u32[]{:S(2)}) copy-start(bf16[1,1,576,128,128]{4,3,2,1,0:T(8,128)(2,1)} %param.12) | copy-start | bytes 56623108
  23.0 6.2 %collective-permute-start.1 = (bf16[8,3072]{1,0:T(8,128)(2,1)}, bf16[8,3072]{1,0:T(8,128)(2,1)S(1)}, u32[]{:S(2)}, u32[]{:S(2)}) collective-permute-start(bf16[8,3072]{1,0:T(8,128)(2,1)} %param.10), channel_id=1, source_target_pairs={{0,4},{2,6},{4,8},{6,10},{8,12},{10,14},{12,0},{14,2},{1,5},{3,7},... | collective-permute-start | bytes 147464 | tf_op jit(solution)/shard_map/ppermute | solution.py:256
  29.2 7.0 %collective-permute-start.15 = (bf16[8,3072]{1,0:T(8,128)(2,1)}, bf16[8,3072]{1,0:T(8,128)(2,1)S(1)}, u32[]{:S(2)}, u32[]{:S(2)}) collective-permute-start(bf16[8,3072]{1,0:T(8,128)(2,1)} %param.11), channel_id=1, source_target_pairs={{0,2},{2,4},{4,6},{6,8},{8,10},{10,12},{12,14},{14,0},{1,3},{3,5},... | collective-permute-start | bytes 147464 | tf_op jit(solution)/shard_map/ppermute | solution.py:256
  36.2 6.1 %collective-permute-start.16 = (bf16[8,3072]{1,0:T(8,128)(2,1)}, bf16[8,3072]{1,0:T(8,128)(2,1)S(1)}, u32[]{:S(2)}, u32[]{:S(2)}) collective-permute-start(bf16[8,3072]{1,0:T(8,128)(2,1)} %param.11), channel_id=1, source_target_pairs={{0,4},{2,6},{4,8},{6,10},{8,12},{10,14},{12,0},{14,2},{1,5},{3,7},... | collective-permute-start | bytes 147464 | tf_op jit(solution)/shard_map/ppermute | solution.py:256
  42.3 6.3 %collective-permute-start.17 = (bf16[8,3072]{1,0:T(8,128)(2,1)}, bf16[8,3072]{1,0:T(8,128)(2,1)S(1)}, u32[]{:S(2)}, u32[]{:S(2)}) collective-permute-start(bf16[8,3072]{1,0:T(8,128)(2,1)} %param.11), channel_id=1, source_target_pairs={{0,6},{2,8},{4,10},{6,12},{8,14},{10,0},{12,2},{14,4},{1,7},{3,9},... | collective-permute-start | bytes 147464 | tf_op jit(solution)/shard_map/ppermute | solution.py:256
  48.6 5.2 %collective-permute-start.18 = (bf16[8,3072]{1,0:T(8,128)(2,1)}, bf16[8,3072]{1,0:T(8,128)(2,1)S(1)}, u32[]{:S(2)}, u32[]{:S(2)}) collective-permute-start(bf16[8,3072]{1,0:T(8,128)(2,1)} %param.11), channel_id=1, source_target_pairs={{0,8},{2,10},{4,12},{6,14},{8,0},{10,2},{12,4},{14,6},{1,9},{3,11}... | collective-permute-start | bytes 147464 | tf_op jit(solution)/shard_map/ppermute | solution.py:256
  53.8 5.2 %collective-permute-start.19 = (bf16[8,3072]{1,0:T(8,128)(2,1)}, bf16[8,3072]{1,0:T(8,128)(2,1)S(1)}, u32[]{:S(2)}, u32[]{:S(2)}) collective-permute-start(bf16[8,3072]{1,0:T(8,128)(2,1)} %param.11), channel_id=1, source_target_pairs={{0,10},{2,12},{4,14},{6,0},{8,2},{10,4},{12,6},{14,8},{1,11},{3,13... | collective-permute-start | bytes 147464 | tf_op jit(solution)/shard_map/ppermute | solution.py:256
  59.0 4.3 %collective-permute-start.20 = (bf16[8,3072]{1,0:T(8,128)(2,1)}, bf16[8,3072]{1,0:T(8,128)(2,1)S(1)}, u32[]{:S(2)}, u32[]{:S(2)}) collective-permute-start(bf16[8,3072]{1,0:T(8,128)(2,1)} %param.11), channel_id=1, source_target_pairs={{0,12},{2,14},{4,0},{6,2},{8,4},{10,6},{12,8},{14,10},{1,13},{3,15... | collective-permute-start | bytes 147464 | tf_op jit(solution)/shard_map/ppermute | solution.py:256
  63.3 4.3 %collective-permute-start.21 = (bf16[8,3072]{1,0:T(8,128)(2,1)}, bf16[8,3072]{1,0:T(8,128)(2,1)S(1)}, u32[]{:S(2)}, u32[]{:S(2)}) collective-permute-start(bf16[8,3072]{1,0:T(8,128)(2,1)} %param.11), channel_id=1, source_target_pairs={{0,14},{2,0},{4,2},{6,4},{8,6},{10,8},{12,10},{14,12},{1,15},{3,1}... | collective-permute-start | bytes 147464 | tf_op jit(solution)/shard_map/ppermute | solution.py:256
  67.6 19.6 %collective-permute-start.6 = (bf16[8,3072]{1,0:T(8,128)(2,1)}, bf16[8,3072]{1,0:T(8,128)(2,1)S(1)}, u32[]{:S(2)}, u32[]{:S(2)}) collective-permute-start(bf16[8,3072]{1,0:T(8,128)(2,1)} %param.10), channel_id=1, source_target_pairs={{0,14},{2,0},{4,2},{6,4},{8,6},{10,8},{12,10},{14,12},{1,15},{3,1}... | collective-permute-start | bytes 147464 | tf_op jit(solution)/shard_map/ppermute | solution.py:256
  87.0 6.7 %collective-permute-start.22 = (bf16[64,3072]{1,0:T(8,128)(2,1)S(1)}, bf16[64,3072]{1,0:T(8,128)(2,1)S(1)}, u32[]{:S(2)}, u32[]{:S(2)}) collective-permute-start(bf16[64,3072]{1,0:T(8,128)(2,1)S(1)} %get-tuple-element.41), channel_id=1, source_target_pairs={{0,1},{1,0},{2,3},{3,2},{4,5},{5,4},{6,7},{7,6},{8,9},{9,8},{10,11... | collective-permute-start | bytes 1179656 | tf_op jit(solution)/shard_map/ppermute | solution.py:272
  93.1 1.9 %collective-permute-start.7 = (bf16[64,3072]{1,0:T(8,128)(2,1)S(1)}, bf16[64,3072]{1,0:T(8,128)(2,1)S(1)}, u32[]{:S(2)}, u32[]{:S(2)}) collective-permute-start(bf16[64,3072]{1,0:T(8,128)(2,1)S(1)} %get-tuple-element.31), channel_id=1, source_target_pairs={{0,1},{1,0},{2,3},{3,2},{4,5},{5,4},{6,7},{7,6},{8,9},{9,8},{10,11... | collective-permute-start | bytes 1179656 | tf_op jit(solution)/shard_map/ppermute | solution.py:272
  95.0 21.8 %copy-start.3 = (s32[576]{0:T(1024)S(1)}, s32[576]{0:T(1024)}, u32[]{:S(2)}) copy-start(s32[576]{0:T(1024)} %get-tuple-element.28.slots) | copy-start | bytes 6916
  103.6 19.7 %collective-permute-start.23 = (bf16[8,3072]{1,0:T(8,128)(2,1)S(1)}, bf16[8,3072]{1,0:T(8,128)(2,1)S(1)}, u32[]{:S(2)}, u32[]{:S(2)}) collective-permute-start(bf16[8,3072]{1,0:T(8,128)(2,1)S(1)} %get-tuple-element.43), channel_id=1, source_target_pairs={{0,14},{2,0},{4,2},{6,4},{8,6},{10,8},{12,10},{14,12},{1,15},{3,1}... | collective-permute-start | bytes 147464 | tf_op jit(solution)/shard_map/ppermute | solution.py:267
  104.5 20.7 %collective-permute-start.24 = (bf16[8,3072]{1,0:T(8,128)(2,1)S(1)}, bf16[8,3072]{1,0:T(8,128)(2,1)S(1)}, u32[]{:S(2)}, u32[]{:S(2)}) collective-permute-start(bf16[8,3072]{1,0:T(8,128)(2,1)S(1)} %get-tuple-element.44), channel_id=1, source_target_pairs={{0,12},{2,14},{4,0},{6,2},{8,4},{10,6},{12,8},{14,10},{1,13},{3,15... | collective-permute-start | bytes 147464 | tf_op jit(solution)/shard_map/ppermute | solution.py:267
  104.5 22.1 %collective-permute-start.25 = (bf16[8,3072]{1,0:T(8,128)(2,1)S(1)}, bf16[8,3072]{1,0:T(8,128)(2,1)S(1)}, u32[]{:S(2)}, u32[]{:S(2)}) collective-permute-start(bf16[8,3072]{1,0:T(8,128)(2,1)S(1)} %get-tuple-element.45), channel_id=1, source_target_pairs={{0,10},{2,12},{4,14},{6,0},{8,2},{10,4},{12,6},{14,8},{1,11},{3,13... | collective-permute-start | bytes 147464 | tf_op jit(solution)/shard_map/ppermute | solution.py:267
  105.0 24.9 %collective-permute-start.26 = (bf16[8,3072]{1,0:T(8,128)(2,1)S(1)}, bf16[8,3072]{1,0:T(8,128)(2,1)S(1)}, u32[]{:S(2)}, u32[]{:S(2)}) collective-permute-start(bf16[8,3072]{1,0:T(8,128)(2,1)S(1)} %get-tuple-element.46), channel_id=1, source_target_pairs={{0,8},{2,10},{4,12},{6,14},{8,0},{10,2},{12,4},{14,6},{1,9},{3,11}... | collective-permute-start | bytes 147464 | tf_op jit(solution)/shard_map/ppermute | solution.py:267
  108.3 30.8 %collective-permute-start.27 = (bf16[8,3072]{1,0:T(8,128)(2,1)S(1)}, bf16[8,3072]{1,0:T(8,128)(2,1)S(1)}, u32[]{:S(2)}, u32[]{:S(2)}) collective-permute-start(bf16[8,3072]{1,0:T(8,128)(2,1)S(1)} %get-tuple-element.47), channel_id=1, source_target_pairs={{0,6},{2,8},{4,10},{6,12},{8,14},{10,0},{12,2},{14,4},{1,7},{3,9},... | collective-permute-start | bytes 147464 | tf_op jit(solution)/shard_map/ppermute | solution.py:267
  123.3 16.4 %collective-permute-start.28 = (bf16[8,3072]{1,0:T(8,128)(2,1)S(1)}, bf16[8,3072]{1,0:T(8,128)(2,1)S(1)}, u32[]{:S(2)}, u32[]{:S(2)}) collective-permute-start(bf16[8,3072]{1,0:T(8,128)(2,1)S(1)} %get-tuple-element.48), channel_id=1, source_target_pairs={{0,4},{2,6},{4,8},{6,10},{8,12},{10,14},{12,0},{14,2},{1,5},{3,7},... | collective-permute-start | bytes 147464 | tf_op jit(solution)/shard_map/ppermute | solution.py:267
  125.2 16.7 %collective-permute-start.29 = (bf16[8,3072]{1,0:T(8,128)(2,1)S(1)}, bf16[8,3072]{1,0:T(8,128)(2,1)S(1)}, u32[]{:S(2)}, u32[]{:S(2)}) collective-permute-start(bf16[8,3072]{1,0:T(8,128)(2,1)S(1)} %get-tuple-element.49), channel_id=1, source_target_pairs={{0,2},{2,4},{4,6},{6,8},{8,10},{10,12},{12,14},{14,0},{1,3},{3,5},... | collective-permute-start | bytes 147464 | tf_op jit(solution)/shard_map/ppermute | solution.py:267
  126.6 16.0 %collective-permute-start.8 = (bf16[8,3072]{1,0:T(8,128)(2,1)S(1)}, bf16[8,3072]{1,0:T(8,128)(2,1)S(1)}, u32[]{:S(2)}, u32[]{:S(2)}) collective-permute-start(bf16[8,3072]{1,0:T(8,128)(2,1)S(1)} %get-tuple-element.33), channel_id=1, source_target_pairs={{0,14},{2,0},{4,2},{6,4},{8,6},{10,8},{12,10},{14,12},{1,15},{3,1}... | collective-permute-start | bytes 147464 | tf_op jit(solution)/shard_map/ppermute | solution.py:267
  129.9 15.6 %collective-permute-start.9 = (bf16[8,3072]{1,0:T(8,128)(2,1)S(1)}, bf16[8,3072]{1,0:T(8,128)(2,1)S(1)}, u32[]{:S(2)}, u32[]{:S(2)}) collective-permute-start(bf16[8,3072]{1,0:T(8,128)(2,1)S(1)} %get-tuple-element.34), channel_id=1, source_target_pairs={{0,12},{2,14},{4,0},{6,2},{8,4},{10,6},{12,8},{14,10},{1,13},{3,15... | collective-permute-start | bytes 147464 | tf_op jit(solution)/shard_map/ppermute | solution.py:267
  139.1 7.4 %collective-permute-start.10 = (bf16[8,3072]{1,0:T(8,128)(2,1)S(1)}, bf16[8,3072]{1,0:T(8,128)(2,1)S(1)}, u32[]{:S(2)}, u32[]{:S(2)}) collective-permute-start(bf16[8,3072]{1,0:T(8,128)(2,1)S(1)} %get-tuple-element.35), channel_id=1, source_target_pairs={{0,10},{2,12},{4,14},{6,0},{8,2},{10,4},{12,6},{14,8},{1,11},{3,13... | collective-permute-start | bytes 147464 | tf_op jit(solution)/shard_map/ppermute | solution.py:267
  139.7 6.8 %collective-permute-start.11 = (bf16[8,3072]{1,0:T(8,128)(2,1)S(1)}, bf16[8,3072]{1,0:T(8,128)(2,1)S(1)}, u32[]{:S(2)}, u32[]{:S(2)}) collective-permute-start(bf16[8,3072]{1,0:T(8,128)(2,1)S(1)} %get-tuple-element.36), channel_id=1, source_target_pairs={{0,8},{2,10},{4,12},{6,14},{8,0},{10,2},{12,4},{14,6},{1,9},{3,11}... | collective-permute-start | bytes 147464 | tf_op jit(solution)/shard_map/ppermute | solution.py:267
  141.9 6.8 %collective-permute-start.12 = (bf16[8,3072]{1,0:T(8,128)(2,1)S(1)}, bf16[8,3072]{1,0:T(8,128)(2,1)S(1)}, u32[]{:S(2)}, u32[]{:S(2)}) collective-permute-start(bf16[8,3072]{1,0:T(8,128)(2,1)S(1)} %get-tuple-element.37), channel_id=1, source_target_pairs={{0,6},{2,8},{4,10},{6,12},{8,14},{10,0},{12,2},{14,4},{1,7},{3,9},... | collective-permute-start | bytes 147464 | tf_op jit(solution)/shard_map/ppermute | solution.py:267
  142.6 6.5 %collective-permute-start.13 = (bf16[8,3072]{1,0:T(8,128)(2,1)S(1)}, bf16[8,3072]{1,0:T(8,128)(2,1)S(1)}, u32[]{:S(2)}, u32[]{:S(2)}) collective-permute-start(bf16[8,3072]{1,0:T(8,128)(2,1)S(1)} %get-tuple-element.38), channel_id=1, source_target_pairs={{0,4},{2,6},{4,8},{6,10},{8,12},{10,14},{12,0},{14,2},{1,5},{3,7},... | collective-permute-start | bytes 147464 | tf_op jit(solution)/shard_map/ppermute | solution.py:267
  145.5 6.8 %collective-permute-start.14 = (bf16[8,3072]{1,0:T(8,128)(2,1)S(1)}, bf16[8,3072]{1,0:T(8,128)(2,1)S(1)}, u32[]{:S(2)}, u32[]{:S(2)}) collective-permute-start(bf16[8,3072]{1,0:T(8,128)(2,1)S(1)} %get-tuple-element.39), channel_id=1, source_target_pairs={{0,2},{2,4},{4,6},{6,8},{8,10},{10,12},{12,14},{14,0},{1,3},{3,5},... | collective-permute-start | bytes 147464 | tf_op jit(solution)/shard_map/ppermute | solution.py:267
  (8 other events, 97.7 us)
where the time goes:
time: 153 us
  Pallas kernels  49.5 us (32%)
  waiting for transfers between devices  46.5 us (30%)
  starting transfers between devices  39.5 us (26%)
  local copies, waits for them, and re-layouts  8.78 us (6%)
  other arithmetic  6.5 us (4%)
  between operations  2.21 us (1%)
    ppermute x14, waiting for transfers between devices, gather(): pieces.append(lax.ppermute(values, 'dp', path))  39.4 us
    ppermute x14, starting transfers between devices, gather(): pieces.append(lax.ppermute(values, 'dp', path))  20 us
    ppermute x14, starting transfers between devices, scatter(): total = total + lax.ppermute(parts[away], 'dp', path).astype(jnp.float32)  18.9 us
    pallas_call x2, Pallas kernels, outer_product(): pl.pallas_call(functools.partial(outer_kernel, tall, wide), out_shape=jax...  16.8 us
    pallas_call x2, Pallas kernels, second_product(): pl.pallas_call(functools.partial(body, depth, width, rows), out_shape=tup...  15 us
    pallas_call x2, Pallas kernels, first_product(): pl.pallas_call(functools.partial(first_kernel, depth, width, across), out...  13.9 us
    unnamed x34, local copies, waits for them, and re-layouts  8.77 us
    ppermute x14, waiting for transfers between devices, scatter(): total = total + lax.ppermute(parts[away], 'dp', path).astype(jnp.float32)  5.8 us
  transfers between devices with their start and end apart: 30, of which 12 were waited for; matrix products, arithmetic and copies ran while one was open for 5% of the time, Pallas kernels for 27%

commit v1 on v0

v1 whole, which is shorter than its diff:
```python
import functools

import jax
import jax.numpy as jnp
from jax import lax
from jax.experimental import pallas as pl
from jax.experimental.pallas import tpu as pltpu
from jax.sharding import PartitionSpec as P

root_half = 0.7071067811865476
inv_root_tau = 0.3989422804014327

SMEM = pl.BlockSpec(memory_space=pltpu.SMEM)
VMEM = pl.BlockSpec(memory_space=pltpu.VMEM)
ANY = pl.BlockSpec(memory_space=pl.ANY)
HBM = pl.BlockSpec(memory_space=pltpu.HBM)
GRANT = 4 << 20


def gelu_curve(values):
    return 0.5 * values * (1.0 + lax.erf(values * root_half))


def gelu_slope(values):
    return (
        0.5 * (1.0 + lax.erf(values * root_half))
        + values * jnp.exp(-0.5 * values * values) * inv_root_tau
    )


def slots_kernel(width, rows, cols, earlier, slots, rows_near, cols_near, sems):
    copies = [
        pltpu.make_async_copy(rows, rows_near, sems.at[0]),
        pltpu.make_async_copy(cols, cols_near, sems.at[1]),
    ]
    for copy in copies:
        copy.start()
    for copy in copies:
        copy.wait()

    def place(slot, carry):
        slots[rows_near[0, 0, slot] * width + cols_near[0, 0, slot]] = slot
        return carry

    lax.fori_loop(0, rows.shape[2], place, 0, unroll=16 if rows.shape[2] % 16 == 0 else 8)


def slot_map(rows, cols, width, earlier, name):
    return pl.pallas_call(
        functools.partial(slots_kernel, width),
        out_shape=jax.ShapeDtypeStruct(rows.shape[2:], jnp.int32),
        in_specs=[HBM, HBM, ANY],
        out_specs=SMEM,
        scratch_shapes=[
            pltpu.SMEM(rows.shape, rows.dtype),
            pltpu.SMEM(cols.shape, cols.dtype),
            pltpu.SemaphoreType.DMA((2,)),
        ],
        compiler_params=pltpu.CompilerParams(vmem_limit_bytes=GRANT),
        cost_estimate=pl.CostEstimate(flops=0, bytes_accessed=6 << 20, transcendentals=0),
        name=name,
    )(in_hbm(rows), in_hbm(cols), earlier)


def pair(count):
    return 2 if count % 2 == 0 else 1


def product(lhs_ref, block, side, depth, deep, wide, across):
    total = None
    for k0 in range(0, depth, deep):
        if across:
            tile = jnp.concatenate(
                [jnp.concatenate([block(k0 + k, n) for k in range(deep)], axis=1) for n in range(wide)],
                axis=0,
            )
            dims = (((1,), (1,)), ((), ()))
        else:
            tile = jnp.concatenate(
                [jnp.concatenate([block(k0 + k, n) for n in range(wide)], axis=1) for k in range(deep)],
                axis=0,
            )
            dims = (((1,), (0,)), ((), ()))
        lhs = lhs_ref[:, k0 * side : (k0 + deep) * side]
        part = lax.dot_general(lhs, tile, dims, preferred_element_type=jnp.float32)
        total = part if total is None else total + part
    return total


def multiply(lhs_ref, blocks_ref, slots_ref, kept, depth, width, across, store):
    side = blocks_ref.shape[-1]
    deep, wide = pair(depth), pair(width)

    def column(step, carry):
        n0 = step * wide

        def block(k, n):
            slot = slots_ref[(n0 + n) * depth + k if across else k * width + n0 + n]
            found = blocks_ref[slot]
            return jnp.where(slot < kept, found, jnp.zeros_like(found))

        total = product(lhs_ref, block, side, depth, deep, wide, across)
        store(pl.multiple_of(n0 * side, wide * side), wide * side, total)
        return carry

    steps = width // wide
    lax.fori_loop(0, steps, column, 0, unroll=pair(steps))


def stream(lhs_ref, blocks_ref, slots_ref, kept, depth, width, across, store, fetched, sems):
    side = blocks_ref.shape[-1]
    deep = pair(depth)
    buffers = fetched.shape[0]
    wide = fetched.shape[1] // depth
    steps = width // wide

    def slot(step, k, n):
        column = step * wide + n
        return slots_ref[column * depth + k if across else k * width + column]

    def fetch(step, buffer):
        for n in range(wide):
            for k in range(depth):
                pltpu.make_async_copy(
                    blocks_ref.at[slot(step, k, n)], fetched.at[buffer, k * wide + n], sems.at[buffer]
                ).start()

    def column(step, buffer):
        pltpu.make_async_copy(
            blocks_ref.at[pl.ds(0, depth * wide)], fetched.at[buffer], sems.at[buffer]
        ).wait()

        def block(k, n):
            found = fetched[buffer, k * wide + n]
            return jnp.where(slot(step, k, n) < kept, found, jnp.zeros_like(found))

        store(
            pl.multiple_of(step * wide * side, wide * side),
            wide * side,
            product(lhs_ref, block, side, depth, deep, wide, across),
        )

    ahead = buffers - 1
    for step in range(ahead):
        fetch(step, step)

    def both(step, carry):
        fetch(step + ahead, lax.rem(step + ahead, buffers))
        column(step, lax.rem(step, buffers))
        return carry

    lax.fori_loop(0, steps - ahead, both, 0)
    for step in range(steps - ahead, steps):
        column(step, step % buffers)


def first_kernel(depth, width, across, slots, kept, lhs, blocks, earlier, own, sent, *fetch):
    def store(start, size, total):
        own[:, pl.ds(start, size)] = total
        sent[:, pl.ds(start, size)] = total.astype(jnp.bfloat16)

    run = stream if fetch else multiply
    run(lhs, blocks, slots, kept[0, 0], depth, width, across, store, *fetch)


def first_product(slots, kept, lhs, blocks, earlier, depth, width, across, streamed, name):
    side = blocks.shape[-1]
    shape = (lhs.shape[0], width * side)
    scratch, grant = [], GRANT
    if streamed:
        wide = next(size for size in (4, 3, 2, 1) if width % size == 0)
        buffers = min(3, width // wide)
        scratch = [
            pltpu.VMEM((buffers, depth * wide, side, side), blocks.dtype),
            pltpu.SemaphoreType.DMA((buffers,)),
        ]
        grant = 16 << 20
    return pl.pallas_call(
        functools.partial(first_kernel, depth, width, across),
        out_shape=(jax.ShapeDtypeStruct(shape, jnp.float32), jax.ShapeDtypeStruct(shape, jnp.bfloat16)),
        in_specs=[SMEM, SMEM, VMEM, HBM if streamed else VMEM, ANY],
        out_specs=(VMEM, VMEM),
        scratch_shapes=scratch,
        compiler_params=pltpu.CompilerParams(vmem_limit_bytes=grant),
        cost_estimate=pl.CostEstimate(
            flops=2 * lhs.size * width * side, bytes_accessed=2 * blocks.size, transcendentals=0
        ),
        name=name,
    )(slots, kept, lhs, in_hbm(blocks) if streamed else in_vmem(blocks), earlier)


def in_hbm(values):
    return pltpu.with_memory_space_constraint(values, pltpu.HBM)


def in_vmem(blocks):
    return pltpu.with_memory_space_constraint(blocks, pltpu.VMEM)


def spread(parts, rows, start_row):
    def store(start, size, total):
        rounded = total.astype(jnp.bfloat16)
        for index, part in enumerate(parts):
            part[start_row : start_row + rows, pl.ds(start, size)] = rounded[index * rows : (index + 1) * rows]

    return store


def output_kernel(depth, width, rows, slots, kept, own, other, blocks, earlier, activated, *parts):
    side = blocks.shape[-1]

    def activate(step, carry):
        at = pl.ds(pl.multiple_of(step * side, side), side)
        hidden = own[:, at] + other[:, at].astype(jnp.float32)
        activated[:, at] = gelu_curve(hidden).astype(jnp.bfloat16)
        return carry

    lax.fori_loop(0, depth, activate, 0)
    multiply(activated, blocks, slots, kept[0, 0], depth, width, False, spread(parts, rows, 0))


def output_product(slots, kept, own, other, blocks, earlier, depth, width, pieces):
    count = own.shape[0]
    side = blocks.shape[-1]
    rows = count // pieces
    shapes = [jax.ShapeDtypeStruct((count, depth * side), jnp.bfloat16)]
    shapes += [jax.ShapeDtypeStruct((rows, width * side), jnp.bfloat16)] * pieces
    activated, *parts = pl.pallas_call(
        functools.partial(output_kernel, depth, width, rows),
        out_shape=tuple(shapes),
        in_specs=[SMEM, SMEM, VMEM, VMEM, VMEM, ANY],
        out_specs=(VMEM,) * len(shapes),
        compiler_params=pltpu.CompilerParams(vmem_limit_bytes=GRANT),
        cost_estimate=pl.CostEstimate(
            flops=2 * count * depth * width * side * side, bytes_accessed=2 * blocks.size, transcendentals=0
        ),
        name="output",
    )(slots, kept, own, other, in_vmem(blocks), earlier)
    return activated, parts


def gradient_kernel(depth, width, rows, pieces, slots, kept, hid_own, hid_other, act_own, act_other, blocks, *refs):
    out_parts, (grad_hidden, *both) = refs[:pieces], refs[pieces:]
    side = blocks.shape[-1]

    def activate(step, carry):
        at = pl.ds(pl.multiple_of(step * side, side), side)
        hidden = hid_own[:, at] + hid_other[:, at].astype(jnp.float32)
        grad_act = act_own[:, at] + act_other[:, at].astype(jnp.float32)
        grad_hidden[:, at] = (grad_act * gelu_slope(hidden)).astype(jnp.bfloat16)
        return carry

    lax.fori_loop(0, depth, activate, 0)
    for part, out_part in zip(both, out_parts):
        part[:rows] = out_part[...]
    multiply(grad_hidden, blocks, slots, kept[0, 0], depth, width, True, spread(both, rows, rows))


def gradient_product(slots, kept, values, blocks, out_parts, depth, width):
    count = values[0].shape[0]
    side = blocks.shape[-1]
    pieces = len(out_parts)
    rows = count // pieces
    shapes = [jax.ShapeDtypeStruct((count, depth * side), jnp.bfloat16)]
    shapes += [jax.ShapeDtypeStruct((2 * rows, width * side), jnp.bfloat16)] * pieces
    grad_hidden, *both = pl.pallas_call(
        functools.partial(gradient_kernel, depth, width, rows, pieces),
        out_shape=tuple(shapes),
        in_specs=[SMEM, SMEM] + [VMEM] * (5 + pieces),
        out_specs=(VMEM,) * len(shapes),
        compiler_params=pltpu.CompilerParams(vmem_limit_bytes=GRANT),
        cost_estimate=pl.CostEstimate(
            flops=2 * count * depth * width * side * side, bytes_accessed=2 * blocks.size, transcendentals=0
        ),
        name="grad_tokens",
    )(slots, kept, *values, in_vmem(blocks), *out_parts)
    return grad_hidden, both


def outer_kernel(tall, wide, slots, kept_ref, left, right, earlier, result, turned, stage, sems):
    count = left.shape[0]
    side = result.shape[-1]
    step_width = stage.shape[1] // tall
    steps = wide // step_width
    buffers = stage.shape[0]
    kept = kept_ref[0, 0]
    scale = float(count) ** (-0.5)
    zero_at = tall * step_width

    for a in range(tall):
        turned[a] = left[:, a * side : (a + 1) * side].T
    for buffer in range(buffers):
        stage[buffer, zero_at] = jnp.zeros((side, side), jnp.bfloat16)

    def wait(buffer):
        pltpu.make_async_copy(
            stage.at[buffer, pl.ds(0, zero_at)], result.at[pl.ds(0, zero_at)], sems.at[buffer]
        ).wait()

    def step(index, carry):
        buffer = lax.rem(index, buffers)

        @pl.when(index >= buffers)
        def _():
            wait(buffer)

        at = pl.ds(pl.multiple_of(index * step_width * side, step_width * side), step_width * side)
        values = right[:, at]
        for a in range(tall):
            tile = jnp.dot(turned[a], values, preferred_element_type=jnp.float32) * scale
            tile = tile.astype(jnp.bfloat16)
            for b in range(step_width):
                stage[buffer, a * step_width + b] = tile[:, b * side : (b + 1) * side]
                slot = slots[a * wide + index * step_width + b]
                source = jnp.where(slot < kept, a * step_width + b, zero_at)
                pltpu.make_async_copy(
                    stage.at[buffer, source], result.at[slot], sems.at[buffer]
                ).start()
        return carry

    lax.fori_loop(0, steps, step, 0)
    for index in range(max(0, steps - buffers), steps):
        wait(index % buffers)


def outer_product(slots, kept, left, right, side, earlier, name):
    count = left.shape[0]
    tall, wide = left.shape[1] // side, right.shape[1] // side
    step_width = next(size for size in (6, 4, 3, 2, 1) if wide % size == 0)
    buffers = min(2, wide // step_width)
    return pl.pallas_call(
        functools.partial(outer_kernel, tall, wide),
        out_shape=jax.ShapeDtypeStruct((tall * wide, side, side), jnp.bfloat16),
        in_specs=[SMEM, SMEM, VMEM, VMEM, ANY],
        out_specs=ANY,
        scratch_shapes=[
            pltpu.VMEM((tall, side, count), jnp.bfloat16),
            pltpu.VMEM((buffers, tall * step_width + 1, side, side), jnp.bfloat16),
            pltpu.SemaphoreType.DMA((buffers,)),
        ],
        compiler_params=pltpu.CompilerParams(vmem_limit_bytes=16 << 20),
        cost_estimate=pl.CostEstimate(
            flops=8 * left.size * right.shape[1],
            bytes_accessed=2 * tall * wide * side * side,
            transcendentals=0,
        ),
        name=name,
    )(slots, kept, left, right, earlier)


def exchange(values, away, devices):
    return lax.ppermute(values, "dp", [(i, i ^ away) for i in range(devices)])


def gather(values, devices):
    if devices != 8:
        return lax.all_gather(values, "dp", axis=0, tiled=True), values
    near = jnp.concatenate([values, exchange(values, 4, devices)], axis=0)
    rest = [exchange(near, away, devices) for away in (2, 3, 1)]
    return jnp.concatenate([near] + rest, axis=0), near


def near_sum(parts, devices):
    total = parts[0].astype(jnp.float32)
    for part, away in zip(parts[1:], (2, 3, 1)):
        total = total + exchange(part, away, devices).astype(jnp.float32)
    return total


def far_sum(total, rows, devices):
    mine = [total[0:rows], total[2 * rows : 3 * rows]]
    theirs = jnp.concatenate([total[rows : 2 * rows], total[3 * rows :]], axis=0).astype(jnp.bfloat16)
    far = exchange(theirs, 4, devices).astype(jnp.float32)
    return [(mine[i] + far[i * rows : (i + 1) * rows]).astype(jnp.bfloat16) for i in range(2)]


def full_sum(both, rows):
    results = []
    for first in (0, rows):
        whole = jnp.concatenate([part[first : first + rows] for part in both], axis=0)
        summed = lax.psum_scatter(whole.astype(jnp.float32), "dp", scatter_dimension=0, tiled=True)
        results.append(summed.astype(jnp.bfloat16))
    return results


def swap(values, devices):
    return lax.ppermute(values, "mp", [(i, (i + 1) % devices) for i in range(devices)])


def shards(
    tokens,
    cotangent,
    inward_blocks,
    inward_rows,
    inward_cols,
    inward_count,
    outward_blocks,
    outward_rows,
    outward_cols,
    outward_count,
):
    side = inward_blocks.shape[-1]
    region = inward_blocks.shape[2]
    row_blocks = tokens.shape[1] // side
    col_blocks = region // row_blocks
    n_dp = lax.axis_size("dp")
    n_mp = lax.axis_size("mp")
    pieces = 4 if n_dp == 8 else n_dp
    in_kept, out_kept = inward_count, outward_count
    inward = inward_blocks.reshape(region, side, side)
    outward = outward_blocks.reshape(region, side, side)
    in_slots = slot_map(inward_rows, inward_cols, col_blocks, in_kept, "in_slots")
    all_tokens, near = gather(tokens, n_dp)
    all_grads, _ = gather(cotangent, n_dp)
    out_slots = slot_map(outward_rows, outward_cols, row_blocks, near, "out_slots")
    hid_own, hid_sent = first_product(
        in_slots, in_kept, all_tokens, inward, in_kept, row_blocks, col_blocks, False, True, "hidden"
    )
    hid_other = swap(hid_sent, n_mp)
    act_own, act_sent = first_product(
        out_slots, out_kept, all_grads, outward, hid_own, row_blocks, col_blocks, True, False, "grad_act"
    )
    act_other = swap(act_sent, n_mp)
    activated, out_parts = output_product(
        out_slots, out_kept, hid_own, hid_other, outward, act_own, col_blocks, row_blocks, pieces
    )
    grad_hidden, both = gradient_product(
        in_slots, in_kept, (hid_own, hid_other, act_own, act_other), inward, out_parts, col_blocks, row_blocks
    )
    rows = tokens.shape[0]
    nearly = near_sum(both, n_dp) if n_dp == 8 else in_kept
    grad_outward = outer_product(out_slots, out_kept, activated, all_grads, side, grad_hidden, "outward")
    grad_inward = outer_product(in_slots, in_kept, all_tokens, grad_hidden, side, nearly, "inward")
    out_tokens, grad_tokens = far_sum(nearly, rows, n_dp) if n_dp == 8 else full_sum(both, rows)
    return (
        out_tokens,
        grad_tokens,
        grad_inward.reshape(inward_blocks.shape),
        grad_outward.reshape(outward_blocks.shape),
    )


def solution(mesh):
    in_specs = (
        P(("sweep", "dp"), "mp"),
        P(("sweep", "dp"), "mp"),
        P(("sweep", "mp"), "dp", None, None, None),
        P(("sweep", "mp"), "dp", None),
        P(("sweep", "mp"), "dp", None),
        P(("sweep", "mp"), "dp"),
        P(("sweep", "dp"), "mp", None, None, None),
        P(("sweep", "dp"), "mp", None),
        P(("sweep", "dp"), "mp", None),
        P(("sweep", "dp"), "mp"),
    )
    out_specs = (
        P(("sweep", "dp"), "mp"),
        P(("sweep", "dp"), "mp"),
        P(("sweep", "mp"), "dp", None, None, None),
        P(("sweep", "dp"), "mp", None, None, None),
    )
    return jax.shard_map(shards, mesh=mesh, in_specs=in_specs, out_specs=out_specs, check_vma=False)
```

time: 153 us -> 75.5 us (0.49)
  waiting for transfers between devices: 46.5 us -> 2.78 us
  starting transfers between devices: 39.5 us -> 19.3 us
  local copies, waits for them, and re-layouts: 8.78 us -> 2.46 us
  other arithmetic: 6.5 us -> 0.78 us
  Pallas kernels: 49.5 us -> 47.7 us
    ppermute x28 -> x12, waiting for transfers between devices: 45.2 us -> 2.78 us  [exchange(): return lax.ppermute(values, 'dp', [(i, i ^ away) for i in range(devices)])]
    ppermute x28 -> x12, starting transfers between devices: 38.9 us -> 18.6 us  [exchange(): return lax.ppermute(values, 'dp', [(i, i ^ away) for i in range(devices)])]
    unnamed x34 -> x18, local copies, waits for them, and re-layouts: 8.77 us -> 2.42 us
    unnamed x5 -> x1, other arithmetic: 5.15 us -> 0.01 us
    pallas_call x2, Pallas kernels: 16.8 us -> 14.5 us  [outer_product(): pl.pallas_call(functools.partial(outer_kernel, tall, wide), out_shape=jax...]
    pallas_call x3 -> x4, Pallas kernels: 18.9 us -> 18.4 us  [the longest x1 7.76 us: gradient_product(): pl.pallas_call(functools.partial(gradient_kernel, depth, width, rows, pie...]
  transfers between devices with their start and end apart: 30 -> 14, of which waited for: 12 -> 2; matrix products, arithmetic and copies ran while one was open for 5% -> 3% of each run, Pallas kernels for 27% -> 53%
where the time goes in v1:
time: 75.5 us; the launch traced here: 75.2 us
  Pallas kernels  47.7 us (63%)
  starting transfers between devices  19.3 us (26%)
  waiting for transfers between devices  2.78 us (4%)
  local copies, waits for them, and re-layouts  2.46 us (3%)
  between operations  2.25 us (3%)
  other arithmetic  0.78 us (1%)
    ppermute x12, starting transfers between devices, exchange(): return lax.ppermute(values, 'dp', [(i, i ^ away) for i in range(devices)])  18.6 us
    pallas_call x2, Pallas kernels, first_product(): pl.pallas_call(functools.partial(first_kernel, depth, width, across), out...  14.8 us
    pallas_call x2, Pallas kernels, outer_product(): pl.pallas_call(functools.partial(outer_kernel, tall, wide), out_shape=jax...  14.5 us
    pallas_call x1, Pallas kernels, gradient_product(): pl.pallas_call(functools.partial(gradient_kernel, depth, width, rows, pie...  7.76 us
    pallas_call x1, Pallas kernels, output_product(): pl.pallas_call(functools.partial(output_kernel, depth, width, rows), out_...  5.42 us
    pallas_call x2, Pallas kernels, slot_map(): pl.pallas_call(functools.partial(slots_kernel, width), out_shape=jax.Shap...  5.19 us
    ppermute x12, waiting for transfers between devices, exchange(): return lax.ppermute(values, 'dp', [(i, i ^ away) for i in range(devices)])  2.78 us
    unnamed x18, local copies, waits for them, and re-layouts  2.42 us
  transfers between devices with their start and end apart: 14, of which 2 were waited for; matrix products, arithmetic and copies ran while one was open for 3% of the time, Pallas kernels for 53%

profile of v1, /device:TPU:0, one launch (start us, length us, event | category | flops | bytes accessed | tf_op | source)
XLA Modules:
  0.0 75.2 jit_solution(153758882067178407)
XLA Ops:
  0.6 4.1 %collective-permute-start = (bf16[8,3072]{1,0:T(8,128)(2,1)}, bf16[8,3072]{1,0:T(8,128)(2,1)S(1)}, u32[]{:S(2)}, u32[]{:S(2)}) collective-permute-start(bf16[8,3072]{1,0:T(8,128)(2,1)} %param.10), channel_id=1, source_target_pairs={{0,8},{2,10},{4,12},{6,14},{8,0},{10,2},{12,4},{14,6},{1,9},{3,11}... | collective-permute-start | bytes 147464 | tf_op jit(solution)/shard_map/ppermute | solution.py:352
  4.7 0.1 collective-permute-start.5
  4.8 1.6 %constant_dynamic-update-slice_fusion.1 = (bf16[16,3072]{1,0:T(8,128)(2,1)S(1)}, bf16[64,3072]{1,0:T(8,128)(2,1)S(1)}) fusion(bf16[8,3072]{1,0:T(8,128)(2,1)} %param.10), kind=kLoop, calls=%fused_computation.7 | loop fusion | bytes 147456
  6.4 0.8 %constant_dynamic-update-slice_fusion.8 = (bf16[16,3072]{1,0:T(8,128)(2,1)S(1)}, bf16[64,3072]{1,0:T(8,128)(2,1)S(1)}) fusion(bf16[8,3072]{1,0:T(8,128)(2,1)} %param.11), kind=kLoop, calls=%fused_computation.14 | loop fusion | bytes 147456
  8.5 2.6 %in_slots.1.slots = s32[576]{0:T(1024)S(1)} custom-call(s32[1,1,576]{2,1,0:T(1,128)} %rows.2, s32[1,1,576]{2,1,0:T(1,128)} %cols.2, s32[1,1]{1,0:T(1,128)S(6)} %copy.24.earlier.kept.kept_ref), custom_call_target="tpu_custom_call" | custom-call | bytes 6291456 | tf_op jit(solution)/shard_map/in_slots/pallas_call | solution.py:49
  11.1 0.0 collective-permute-done
  11.1 2.1 %collective-permute-start.3 = (bf16[16,3072]{1,0:T(8,128)(2,1)S(1)}, bf16[16,3072]{1,0:T(8,128)(2,1)S(1)}, u32[]{:S(2)}, u32[]{:S(2)}) collective-permute-start(bf16[16,3072]{1,0:T(8,128)(2,1)S(1)} %get-tuple-element.42.earlier), channel_id=1, source_target_pairs={{0,2},{2,0},{4,6},{6,4},{8,10},{10,8},{12,14},{14,12},{1,3},{3,1},... | collective-permute-start | bytes 294920 | tf_op jit(solution)/shard_map/ppermute | solution.py:352
  13.2 1.5 %collective-permute-start.2 = (bf16[16,3072]{1,0:T(8,128)(2,1)S(1)}, bf16[16,3072]{1,0:T(8,128)(2,1)S(1)}, u32[]{:S(2)}, u32[]{:S(2)}) collective-permute-start(bf16[16,3072]{1,0:T(8,128)(2,1)S(1)} %get-tuple-element.42.earlier), channel_id=1, source_target_pairs={{0,6},{2,4},{4,2},{6,0},{8,14},{10,12},{12,10},{14,8},{1,7},{3,5},... | collective-permute-start | bytes 294920 | tf_op jit(solution)/shard_map/ppermute | solution.py:352
  14.8 0.0 collective-permute-start.1
  14.8 2.0 %collective-permute-start.8 = (bf16[16,3072]{1,0:T(8,128)(2,1)S(1)}, bf16[16,3072]{1,0:T(8,128)(2,1)S(1)}, u32[]{:S(2)}, u32[]{:S(2)}) collective-permute-start(bf16[16,3072]{1,0:T(8,128)(2,1)S(1)} %get-tuple-element.38), channel_id=1, source_target_pairs={{0,2},{2,0},{4,6},{6,4},{8,10},{10,8},{12,14},{14,12},{1,3},{3,1},... | collective-permute-start | bytes 294920 | tf_op jit(solution)/shard_map/ppermute | solution.py:352
  16.8 1.5 %collective-permute-start.7 = (bf16[16,3072]{1,0:T(8,128)(2,1)S(1)}, bf16[16,3072]{1,0:T(8,128)(2,1)S(1)}, u32[]{:S(2)}, u32[]{:S(2)}) collective-permute-start(bf16[16,3072]{1,0:T(8,128)(2,1)S(1)} %get-tuple-element.38), channel_id=1, source_target_pairs={{0,6},{2,4},{4,2},{6,0},{8,14},{10,12},{12,10},{14,8},{1,7},{3,5},... | collective-permute-start | bytes 294920 | tf_op jit(solution)/shard_map/ppermute | solution.py:352
  18.4 2.6 %out_slots.1.slots = s32[576]{0:T(1024)S(1)} custom-call(s32[1,1,576]{2,1,0:T(1,128)} %rows.3, s32[1,1,576]{2,1,0:T(1,128)} %cols.3, bf16[16,3072]{1,0:T(8,128)(2,1)S(1)} %get-tuple-element.42.earlier), custom_call_target="tpu_custom_call" | custom-call | bytes 6291456 | tf_op jit(solution)/shard_map/out_slots/pallas_call | solution.py:49
  21.0 1.0 %collective-permute-start.6 = (bf16[16,3072]{1,0:T(8,128)(2,1)S(1)}, bf16[16,3072]{1,0:T(8,128)(2,1)S(1)}, u32[]{:S(2)}, u32[]{:S(2)}) collective-permute-start(bf16[16,3072]{1,0:T(8,128)(2,1)S(1)} %get-tuple-element.38), channel_id=1, source_target_pairs={{0,4},{2,6},{4,0},{6,2},{8,12},{10,14},{12,8},{14,10},{1,5},{3,7},... | collective-permute-start | bytes 294920 | tf_op jit(solution)/shard_map/ppermute | solution.py:352
  22.0 7.8 %hidden.1 = (f32[64,3072]{1,0:T(8,128)S(1)}, bf16[64,3072]{1,0:T(8,128)(2,1)S(1)}) custom-call(s32[576]{0:T(1024)S(1)} %in_slots.1.slots, s32[1,1]{1,0:T(1,128)S(6)} %copy.24.earlier.kept.kept_ref, bf16[64,3072]{1,0:T(8,128)(2,1)S(1)} %constant_dynamic-update-slice_fusion.2.lhs.left, bf16[576,128,128]{2,1,0:T(8,128)(2,1)} %bitcast.6, ...), custom_call_target="tpu_custom_call" | custom-call | flops 1207959552 | bytes 18874368 | tf_op jit(solution)/shard_map/hidden/pallas_call | solution.py:178
  29.8 0.1 collective-permute-start.4
  30.0 0.0 slice-start
  30.0 0.0 slice-start.1
  30.0 0.0 slice-start.2
  30.0 7.1 %grad_act.1 = (f32[64,3072]{1,0:T(8,128)S(1)}, bf16[64,3072]{1,0:T(8,128)(2,1)S(1)}) custom-call(s32[576]{0:T(1024)S(1)} %out_slots.1.slots, s32[1,1]{1,0:T(1,128)S(6)} %copy.25.kept.kept_ref, bf16[64,3072]{1,0:T(8,128)(2,1)S(1)} %constant_dynamic-update-slice_fusion.9.lhs.right, bf16[576,128,128]{2,1,0:T(8,128)(2,1)S(1)} %bitcast.4, ...), custom_call_target="tpu_custom_call" | custom-call | flops 1207959552 | bytes 18874368 | tf_op jit(solution)/shard_map/grad_act/pallas_call | solution.py:178
  37.1 0.5 collective-permute-start.9
  37.7 5.4 %output.1 = (bf16[64,3072]{1,0:T(8,128)(2,1)S(1)}, bf16[16,3072]{1,0:T(8,128)(2,1)S(1)}, bf16[16,3072]{1,0:T(8,128)(2,1)S(1)}, bf16[16,3072]{1,0:T(8,128)(2,1)S(1)}, bf16[16,3072]{1,0:T(8,128)(2,1)S(1)}) custom-call(s32[576]{0:T(1024)S(1)} %out_slots.1.slots, s32[1,1]{1,0:T(1,128)S(6)} %copy.25.kept.kept_ref, ...), custom_call_target="tpu_custom_call" | custom-call | flops 1207959552 | bytes 18874368 | tf_op jit(solution)/shard_map/output/pallas_call | solution.py:228
  43.1 7.8 %grad_tokens.1 = (bf16[64,3072]{1,0:T(8,128)(2,1)S(1)}, bf16[32,3072]{1,0:T(8,128)(2,1)S(1)}, bf16[32,3072]{1,0:T(8,128)(2,1)S(1)}, bf16[32,3072]{1,0:T(8,128)(2,1)S(1)}, bf16[32,3072]{1,0:T(8,128)(2,1)S(1)}) custom-call(s32[576]{0:T(1024)S(1)} %in_slots.1.slots, s32[1,1]{1,0:T(1,128)S(6)} %copy.24.earlier.kept.kept_ref, ...), custom_call_target="tpu_custom_call" | custom-call | flops 1207959552 | bytes 18874368 | tf_op jit(solution)/shard_map/grad_tokens/pallas_call | solution.py:266
  50.9 1.1 %collective-permute-start.10 = (bf16[32,3072]{1,0:T(8,128)(2,1)S(1)}, bf16[32,3072]{1,0:T(8,128)(2,1)S(1)}, u32[]{:S(2)}, u32[]{:S(2)}) collective-permute-start(bf16[32,3072]{1,0:T(8,128)(2,1)S(1)} %get-tuple-element.27), channel_id=1, source_target_pairs={{0,4},{2,6},{4,0},{6,2},{8,12},{10,14},{12,8},{14,10},{1,5},{3,7},... | collective-permute-start | bytes 589832 | tf_op jit(solution)/shard_map/ppermute | solution.py:352
  52.0 1.9 %collective-permute-start.11 = (bf16[32,3072]{1,0:T(8,128)(2,1)S(1)}, bf16[32,3072]{1,0:T(8,128)(2,1)S(1)}, u32[]{:S(2)}, u32[]{:S(2)}) collective-permute-start(bf16[32,3072]{1,0:T(8,128)(2,1)S(1)} %get-tuple-element.28), channel_id=1, source_target_pairs={{0,6},{2,4},{4,2},{6,0},{8,14},{10,12},{12,10},{14,8},{1,7},{3,5},... | collective-permute-start | bytes 589832 | tf_op jit(solution)/shard_map/ppermute | solution.py:352
  54.0 0.5 collective-permute-start.12
  54.5 7.2 %outward.1 = bf16[576,128,128]{2,1,0:T(8,128)(2,1)} custom-call(s32[576]{0:T(1024)S(1)} %out_slots.1.slots, s32[1,1]{1,0:T(1,128)S(6)} %copy.25.kept.kept_ref, bf16[64,3072]{1,0:T(8,128)(2,1)S(1)} %get-tuple-element.31.left, bf16[64,3072]{1,0:T(8,128)(2,1)S(1)} %constant_dynamic-update-slice_fusion.9.lhs.right, ...), custom_call_target="tpu_custom_call" | custom-call | flops 4831838208 | bytes 18874368 | tf_op jit(solution)/shard_map/outward/pallas_call | solution.py:331
  61.7 1.4 %collective-permute-done.11 = bf16[32,3072]{1,0:T(8,128)(2,1)S(1)} collective-permute-done((bf16[32,3072]{1,0:T(8,128)(2,1)S(1)}, bf16[32,3072]{1,0:T(8,128)(2,1)S(1)}, u32[]{:S(2)}, u32[]{:S(2)}) %collective-permute-start.11) | collective-permute-done | bytes 196640 | tf_op jit(solution)/shard_map/ppermute | solution.py:352
  63.1 1.4 %collective-permute-done.12 = bf16[32,3072]{1,0:T(8,128)(2,1)S(1)} collective-permute-done((bf16[32,3072]{1,0:T(8,128)(2,1)S(1)}, bf16[32,3072]{1,0:T(8,128)(2,1)S(1)}, u32[]{:S(2)}, u32[]{:S(2)}) %collective-permute-start.12) | collective-permute-done | bytes 196640 | tf_op jit(solution)/shard_map/ppermute | solution.py:352
  64.5 0.1 fusion.2
  64.6 2.7 %collective-permute-start.13 = (bf16[16,3072]{1,0:T(8,128)(2,1)S(1)}, bf16[16,3072]{1,0:T(8,128)(2,1)S(1)}, u32[]{:S(2)}, u32[]{:S(2)}) collective-permute-start(bf16[16,3072]{1,0:T(8,128)(2,1)S(1)} %pad_maximum_fusion), channel_id=1, source_target_pairs={{0,8},{2,10},{4,12},{6,14},{8,0},{10,2},{12,4},{14,6},{1,9},{3,11}... | collective-permute-start | bytes 294920 | tf_op jit(solution)/shard_map/ppermute | solution.py:352
  67.3 7.2 %inward.1 = bf16[576,128,128]{2,1,0:T(8,128)(2,1)} custom-call(s32[576]{0:T(1024)S(1)} %in_slots.1.slots, s32[1,1]{1,0:T(1,128)S(6)} %copy.24.earlier.kept.kept_ref, bf16[64,3072]{1,0:T(8,128)(2,1)S(1)} %constant_dynamic-update-slice_fusion.2.lhs.left, bf16[64,3072]{1,0:T(8,128)(2,1)S(1)} %get-tuple-element.30.right.earlier, ...), custom_call_target="tpu_custom_call" | custom-call | flops 4831838208 | bytes 18874368 | tf_op jit(solution)/shard_map/inward/pallas_call | solution.py:331
  74.6 0.7 fusion
  (32 shorter events, 0.2 us)
Async XLA Ops:
  0.6 29.4 %copy-start = (bf16[1,1,576,128,128]{4,3,2,1,0:T(8,128)(2,1)S(1)}, bf16[1,1,576,128,128]{4,3,2,1,0:T(8,128)(2,1)}, u32[]{:S(2)}) copy-start(bf16[1,1,576,128,128]{4,3,2,1,0:T(8,128)(2,1)} %param.16) | copy-start | bytes 56623108
  0.6 10.4 %collective-permute-start = (bf16[8,3072]{1,0:T(8,128)(2,1)}, bf16[8,3072]{1,0:T(8,128)(2,1)S(1)}, u32[]{:S(2)}, u32[]{:S(2)}) collective-permute-start(bf16[8,3072]{1,0:T(8,128)(2,1)} %param.10), channel_id=1, source_target_pairs={{0,8},{2,10},{4,12},{6,14},{8,0},{10,2},{12,4},{14,6},{1,9},{3,11}... | collective-permute-start | bytes 147464 | tf_op jit(solution)/shard_map/ppermute | solution.py:352
  4.7 10.1 %collective-permute-start.5 = (bf16[8,3072]{1,0:T(8,128)(2,1)}, bf16[8,3072]{1,0:T(8,128)(2,1)S(1)}, u32[]{:S(2)}, u32[]{:S(2)}) collective-permute-start(bf16[8,3072]{1,0:T(8,128)(2,1)} %param.11), channel_id=1, source_target_pairs={{0,8},{2,10},{4,12},{6,14},{8,0},{10,2},{12,4},{14,6},{1,9},{3,11}... | collective-permute-start | bytes 147464 | tf_op jit(solution)/shard_map/ppermute | solution.py:352
  11.1 10.9 %collective-permute-start.3 = (bf16[16,3072]{1,0:T(8,128)(2,1)S(1)}, bf16[16,3072]{1,0:T(8,128)(2,1)S(1)}, u32[]{:S(2)}, u32[]{:S(2)}) collective-permute-start(bf16[16,3072]{1,0:T(8,128)(2,1)S(1)} %get-tuple-element.42.earlier), channel_id=1, source_target_pairs={{0,2},{2,0},{4,6},{6,4},{8,10},{10,8},{12,14},{14,12},{1,3},{3,1},... | collective-permute-start | bytes 294920 | tf_op jit(solution)/shard_map/ppermute | solution.py:352
  13.2 8.8 %collective-permute-start.2 = (bf16[16,3072]{1,0:T(8,128)(2,1)S(1)}, bf16[16,3072]{1,0:T(8,128)(2,1)S(1)}, u32[]{:S(2)}, u32[]{:S(2)}) collective-permute-start(bf16[16,3072]{1,0:T(8,128)(2,1)S(1)} %get-tuple-element.42.earlier), channel_id=1, source_target_pairs={{0,6},{2,4},{4,2},{6,0},{8,14},{10,12},{12,10},{14,8},{1,7},{3,5},... | collective-permute-start | bytes 294920 | tf_op jit(solution)/shard_map/ppermute | solution.py:352
  14.8 6.2 %collective-permute-start.1 = (bf16[16,3072]{1,0:T(8,128)(2,1)S(1)}, bf16[16,3072]{1,0:T(8,128)(2,1)S(1)}, u32[]{:S(2)}, u32[]{:S(2)}) collective-permute-start(bf16[16,3072]{1,0:T(8,128)(2,1)S(1)} %get-tuple-element.42.earlier), channel_id=1, source_target_pairs={{0,4},{2,6},{4,0},{6,2},{8,12},{10,14},{12,8},{14,10},{1,5},{3,7},... | collective-permute-start | bytes 294920 | tf_op jit(solution)/shard_map/ppermute | solution.py:352
  14.8 15.1 %collective-permute-start.8 = (bf16[16,3072]{1,0:T(8,128)(2,1)S(1)}, bf16[16,3072]{1,0:T(8,128)(2,1)S(1)}, u32[]{:S(2)}, u32[]{:S(2)}) collective-permute-start(bf16[16,3072]{1,0:T(8,128)(2,1)S(1)} %get-tuple-element.38), channel_id=1, source_target_pairs={{0,2},{2,0},{4,6},{6,4},{8,10},{10,8},{12,14},{14,12},{1,3},{3,1},... | collective-permute-start | bytes 294920 | tf_op jit(solution)/shard_map/ppermute | solution.py:352
  16.8 13.1 %collective-permute-start.7 = (bf16[16,3072]{1,0:T(8,128)(2,1)S(1)}, bf16[16,3072]{1,0:T(8,128)(2,1)S(1)}, u32[]{:S(2)}, u32[]{:S(2)}) collective-permute-start(bf16[16,3072]{1,0:T(8,128)(2,1)S(1)} %get-tuple-element.38), channel_id=1, source_target_pairs={{0,6},{2,4},{4,2},{6,0},{8,14},{10,12},{12,10},{14,8},{1,7},{3,5},... | collective-permute-start | bytes 294920 | tf_op jit(solution)/shard_map/ppermute | solution.py:352
  21.0 8.9 %collective-permute-start.6 = (bf16[16,3072]{1,0:T(8,128)(2,1)S(1)}, bf16[16,3072]{1,0:T(8,128)(2,1)S(1)}, u32[]{:S(2)}, u32[]{:S(2)}) collective-permute-start(bf16[16,3072]{1,0:T(8,128)(2,1)S(1)} %get-tuple-element.38), channel_id=1, source_target_pairs={{0,4},{2,6},{4,0},{6,2},{8,12},{10,14},{12,8},{14,10},{1,5},{3,7},... | collective-permute-start | bytes 294920 | tf_op jit(solution)/shard_map/ppermute | solution.py:352
  29.8 7.8 %collective-permute-start.4 = (bf16[64,3072]{1,0:T(8,128)(2,1)S(1)}, bf16[64,3072]{1,0:T(8,128)(2,1)S(1)}, u32[]{:S(2)}, u32[]{:S(2)}) collective-permute-start(bf16[64,3072]{1,0:T(8,128)(2,1)S(1)} %get-tuple-element.19), channel_id=1, source_target_pairs={{0,1},{1,0},{2,3},{3,2},{4,5},{5,4},{6,7},{7,6},{8,9},{9,8},{10,11... | collective-permute-start | bytes 1179656 | tf_op jit(solution)/shard_map/ppermute | solution.py:387
  30.0 13.1 %slice-start = ((s8[18874368]{0:T(1024)(128)(4,1)}), s8[4194304]{0:T(1024)(128)(4,1)S(1)}, s32[]{:S(2)}) async-start(s8[18874368]{0:T(1024)(128)(4,1)} %bitcast.7), calls=%async_computation | async-start | bytes 8388608
  30.0 13.1 %slice-start.1 = ((s8[18874368]{0:T(1024)(128)(4,1)}), s8[4194304]{0:T(1024)(128)(4,1)S(1)}, s32[]{:S(2)}) async-start(s8[18874368]{0:T(1024)(128)(4,1)} %bitcast.7), calls=%async_computation.1 | async-start | bytes 8388608
  30.0 13.1 %slice-start.2 = ((s8[18874368]{0:T(1024)(128)(4,1)}), s8[4194304]{0:T(1024)(128)(4,1)S(1)}, s32[]{:S(2)}) async-start(s8[18874368]{0:T(1024)(128)(4,1)} %bitcast.7), calls=%async_computation.2 | async-start | bytes 8388608
  37.1 6.0 %collective-permute-start.9 = (bf16[64,3072]{1,0:T(8,128)(2,1)S(1)}, bf16[64,3072]{1,0:T(8,128)(2,1)S(1)}, u32[]{:S(2)}, u32[]{:S(2)}) collective-permute-start(bf16[64,3072]{1,0:T(8,128)(2,1)S(1)} %get-tuple-element.21), channel_id=1, source_target_pairs={{0,1},{1,0},{2,3},{3,2},{4,5},{5,4},{6,7},{7,6},{8,9},{9,8},{10,11... | collective-permute-start | bytes 1179656 | tf_op jit(solution)/shard_map/ppermute | solution.py:387
  37.7 5.5 %slice-start.3 = ((s8[18874368]{0:T(1024)(128)(4,1)}), s8[4194304]{0:T(1024)(128)(4,1)S(1)}, s32[]{:S(2)}) async-start(s8[18874368]{0:T(1024)(128)(4,1)} %bitcast.7), calls=%async_computation.3 | async-start | bytes 8388608
  37.7 5.5 %slice-start.4 = ((s8[18874368]{0:T(1024)(128)(4,1)}), s8[2097152]{0:T(1024)(128)(4,1)S(1)}, s32[]{:S(2)}) async-start(s8[18874368]{0:T(1024)(128)(4,1)} %bitcast.7), calls=%async_computation.4 | async-start | bytes 4194304
  50.9 10.8 %collective-permute-start.10 = (bf16[32,3072]{1,0:T(8,128)(2,1)S(1)}, bf16[32,3072]{1,0:T(8,128)(2,1)S(1)}, u32[]{:S(2)}, u32[]{:S(2)}) collective-permute-start(bf16[32,3072]{1,0:T(8,128)(2,1)S(1)} %get-tuple-element.27), channel_id=1, source_target_pairs={{0,4},{2,6},{4,0},{6,2},{8,12},{10,14},{12,8},{14,10},{1,5},{3,7},... | collective-permute-start | bytes 589832 | tf_op jit(solution)/shard_map/ppermute | solution.py:352
  52.0 11.1 %collective-permute-start.11 = (bf16[32,3072]{1,0:T(8,128)(2,1)S(1)}, bf16[32,3072]{1,0:T(8,128)(2,1)S(1)}, u32[]{:S(2)}, u32[]{:S(2)}) collective-permute-start(bf16[32,3072]{1,0:T(8,128)(2,1)S(1)} %get-tuple-element.28), channel_id=1, source_target_pairs={{0,6},{2,4},{4,2},{6,0},{8,14},{10,12},{12,10},{14,8},{1,7},{3,5},... | collective-permute-start | bytes 589832 | tf_op jit(solution)/shard_map/ppermute | solution.py:352
  54.0 10.5 %collective-permute-start.12 = (bf16[32,3072]{1,0:T(8,128)(2,1)S(1)}, bf16[32,3072]{1,0:T(8,128)(2,1)S(1)}, u32[]{:S(2)}, u32[]{:S(2)}) collective-permute-start(bf16[32,3072]{1,0:T(8,128)(2,1)S(1)} %get-tuple-element.29), channel_id=1, source_target_pairs={{0,2},{2,0},{4,6},{6,4},{8,10},{10,8},{12,14},{14,12},{1,3},{3,1},... | collective-permute-start | bytes 589832 | tf_op jit(solution)/shard_map/ppermute | solution.py:352
  64.6 9.9 %collective-permute-start.13 = (bf16[16,3072]{1,0:T(8,128)(2,1)S(1)}, bf16[16,3072]{1,0:T(8,128)(2,1)S(1)}, u32[]{:S(2)}, u32[]{:S(2)}) collective-permute-start(bf16[16,3072]{1,0:T(8,128)(2,1)S(1)} %pad_maximum_fusion), channel_id=1, source_target_pairs={{0,8},{2,10},{4,12},{6,14},{8,0},{10,2},{12,4},{14,6},{1,9},{3,11}... | collective-permute-start | bytes 294920 | tf_op jit(solution)/shard_map/ppermute | solution.py:352

commit v2 on v1

v2 whole, which is shorter than its diff:
```python
import functools

import jax
import jax.numpy as jnp
from jax import lax
from jax.experimental import pallas as pl
from jax.experimental.pallas import tpu as pltpu
from jax.sharding import PartitionSpec as P

root_half = 0.7071067811865476
inv_root_tau = 0.3989422804014327

SMEM = pl.BlockSpec(memory_space=pltpu.SMEM)
VMEM = pl.BlockSpec(memory_space=pltpu.VMEM)
ANY = pl.BlockSpec(memory_space=pl.ANY)
HBM = pl.BlockSpec(memory_space=pltpu.HBM)
GRANT = 4 << 20


def gelu_curve(values):
    return 0.5 * values * (1.0 + lax.erf(values * root_half))


def gelu_slope(values):
    return (
        0.5 * (1.0 + lax.erf(values * root_half))
        + values * jnp.exp(-0.5 * values * values) * inv_root_tau
    )


def slots_kernel(widths, *refs):
    far, counts, slots, near, (spread_out, sems) = refs[:4], refs[4:6], refs[6:8], refs[8:12], refs[12:]
    copies = [pltpu.make_async_copy(*ends, sems.at[index]) for index, ends in enumerate(zip(far, near))]
    for copy in copies:
        copy.start()
    for copy in copies:
        copy.wait()
    region = near[0].shape[-1]
    lanes = spread_out.shape[-1]
    side = 128
    down = lax.broadcasted_iota(jnp.int32, (side, side), 0)
    along = lax.broadcasted_iota(jnp.int32, (side, side), 1)
    positions = lax.broadcasted_iota(jnp.int32, (side, lanes), 1)
    for which, width in enumerate(widths):
        rows, cols, kept = near[2 * which], near[2 * which + 1], counts[which]
        spread_out[...] = jnp.full(spread_out.shape, -1, jnp.int32)
        spread_out[0:1, 0:region] = rows[0] * width + cols[0]
        total = jnp.zeros((1, lanes), jnp.int32)
        for start in range(0, lanes, side):
            there = jnp.broadcast_to(spread_out[0:1, start : start + side], (side, side))
            column = jnp.sum(jnp.where(down == along, there, 0), axis=1, keepdims=True)
            slot = lax.broadcasted_iota(jnp.int32, (side, lanes), 0) + start
            code = jnp.where(slot < kept[0, 0], slot, slot - region)
            total += jnp.sum(jnp.where(column == positions, code, 0), axis=0, keepdims=True)
        slots[which][...] = total[:, 0:region]


def slot_maps(places, counts, in_width, out_width):
    region = places[0].shape[-1]
    lanes = -(-region // 128) * 128
    shape = jax.ShapeDtypeStruct((1, region), jnp.int32)
    near = [pltpu.VMEM(place.shape, place.dtype) for place in places]
    return pl.pallas_call(
        functools.partial(slots_kernel, (in_width, out_width)),
        out_shape=(shape, shape),
        in_specs=[HBM] * 4 + [SMEM] * 2,
        out_specs=(VMEM, VMEM),
        scratch_shapes=near + [pltpu.VMEM((8, lanes), jnp.int32), pltpu.SemaphoreType.DMA((4,))],
        compiler_params=pltpu.CompilerParams(vmem_limit_bytes=GRANT),
        cost_estimate=pl.CostEstimate(flops=0, bytes_accessed=4 << 20, transcendentals=0),
        name="slot_maps",
    )(*[in_hbm(place) for place in places], *counts)


def pair(count):
    return 2 if count % 2 == 0 else 1


def product(lhs_ref, block, side, depth, deep, wide, across):
    total = None
    for k0 in range(0, depth, deep):
        if across:
            tile = jnp.concatenate(
                [jnp.concatenate([block(k0 + k, n) for k in range(deep)], axis=1) for n in range(wide)],
                axis=0,
            )
            dims = (((1,), (1,)), ((), ()))
        else:
            tile = jnp.concatenate(
                [jnp.concatenate([block(k0 + k, n) for n in range(wide)], axis=1) for k in range(deep)],
                axis=0,
            )
            dims = (((1,), (0,)), ((), ()))
        lhs = lhs_ref[:, k0 * side : (k0 + deep) * side]
        part = lax.dot_general(lhs, tile, dims, preferred_element_type=jnp.float32)
        total = part if total is None else total + part
    return total


def multiply(lhs_ref, blocks_ref, slots_ref, depth, width, across, store):
    side = blocks_ref.shape[-1]
    deep, wide = pair(depth), pair(width)

    def column(step, carry):
        n0 = step * wide

        def block(k, n):
            slot = slots_ref[0, (n0 + n) * depth + k if across else k * width + n0 + n]
            found = blocks_ref[jnp.maximum(slot, 0)]
            return jnp.where(slot >= 0, found, jnp.zeros_like(found))

        total = product(lhs_ref, block, side, depth, deep, wide, across)
        store(pl.multiple_of(n0 * side, wide * side), wide * side, total)
        return carry

    steps = width // wide
    lax.fori_loop(0, steps, column, 0, unroll=pair(steps))


def stream(lhs_ref, blocks_ref, slots_ref, depth, width, across, store, fetched, sems):
    side = blocks_ref.shape[-1]
    deep = pair(depth)
    buffers = fetched.shape[0]
    wide = fetched.shape[1] // depth
    steps = width // wide

    def slot(step, k, n):
        column = step * wide + n
        return slots_ref[0, column * depth + k if across else k * width + column]

    def fetch(step, buffer):
        for n in range(wide):
            for k in range(depth):
                code = slot(step, k, n)
                source = jnp.where(code >= 0, code, code + blocks_ref.shape[0])
                pltpu.make_async_copy(
                    blocks_ref.at[source], fetched.at[buffer, k * wide + n], sems.at[buffer]
                ).start()

    def column(step, buffer):
        pltpu.make_async_copy(
            blocks_ref.at[pl.ds(0, depth * wide)], fetched.at[buffer], sems.at[buffer]
        ).wait()

        def block(k, n):
            found = fetched[buffer, k * wide + n]
            return jnp.where(slot(step, k, n) >= 0, found, jnp.zeros_like(found))

        store(
            pl.multiple_of(step * wide * side, wide * side),
            wide * side,
            product(lhs_ref, block, side, depth, deep, wide, across),
        )

    ahead = buffers - 1
    for step in range(ahead):
        fetch(step, step)

    def both(step, carry):
        fetch(step + ahead, lax.rem(step + ahead, buffers))
        column(step, lax.rem(step, buffers))
        return carry

    lax.fori_loop(0, steps - ahead, both, 0)
    for step in range(steps - ahead, steps):
        column(step, step % buffers)


def first_kernel(depth, width, across, slots, lhs, blocks, earlier, own, sent, *fetch):
    def store(start, size, total):
        own[:, pl.ds(start, size)] = total
        sent[:, pl.ds(start, size)] = total.astype(jnp.bfloat16)

    run = stream if fetch else multiply
    run(lhs, blocks, slots, depth, width, across, store, *fetch)


def first_product(slots, lhs, blocks, earlier, depth, width, across, streamed, name):
    side = blocks.shape[-1]
    shape = (lhs.shape[0], width * side)
    scratch, grant = [], GRANT
    if streamed:
        wide = next(size for size in (4, 3, 2, 1) if width % size == 0)
        buffers = min(3, width // wide)
        scratch = [
            pltpu.VMEM((buffers, depth * wide, side, side), blocks.dtype),
            pltpu.SemaphoreType.DMA((buffers,)),
        ]
        grant = 16 << 20
    return pl.pallas_call(
        functools.partial(first_kernel, depth, width, across),
        out_shape=(jax.ShapeDtypeStruct(shape, jnp.float32), jax.ShapeDtypeStruct(shape, jnp.bfloat16)),
        in_specs=[SMEM, VMEM, HBM if streamed else VMEM, ANY],
        out_specs=(VMEM, VMEM),
        scratch_shapes=scratch,
        compiler_params=pltpu.CompilerParams(vmem_limit_bytes=grant),
        cost_estimate=pl.CostEstimate(
            flops=2 * lhs.size * width * side, bytes_accessed=2 * blocks.size, transcendentals=0
        ),
        name=name,
    )(slots, lhs, in_hbm(blocks) if streamed else in_vmem(blocks), earlier)


def in_hbm(values):
    return pltpu.with_memory_space_constraint(values, pltpu.HBM)


def in_vmem(blocks):
    return pltpu.with_memory_space_constraint(blocks, pltpu.VMEM)


def spread(parts, rows, start_row):
    def store(start, size, total):
        rounded = total.astype(jnp.bfloat16)
        for index, part in enumerate(parts):
            part[start_row : start_row + rows, pl.ds(start, size)] = rounded[index * rows : (index + 1) * rows]

    return store


def output_kernel(depth, width, rows, slots, own, other, blocks, earlier, activated, *parts):
    side = blocks.shape[-1]

    def activate(step, carry):
        at = pl.ds(pl.multiple_of(step * side, side), side)
        hidden = own[:, at] + other[:, at].astype(jnp.float32)
        activated[:, at] = gelu_curve(hidden).astype(jnp.bfloat16)
        return carry

    lax.fori_loop(0, depth, activate, 0)
    multiply(activated, blocks, slots, depth, width, False, spread(parts, rows, 0))


def output_product(slots, own, other, blocks, earlier, depth, width, pieces):
    count = own.shape[0]
    side = blocks.shape[-1]
    rows = count // pieces
    shapes = [jax.ShapeDtypeStruct((count, depth * side), jnp.bfloat16)]
    shapes += [jax.ShapeDtypeStruct((rows, width * side), jnp.bfloat16)] * pieces
    activated, *parts = pl.pallas_call(
        functools.partial(output_kernel, depth, width, rows),
        out_shape=tuple(shapes),
        in_specs=[SMEM, VMEM, VMEM, VMEM, ANY],
        out_specs=(VMEM,) * len(shapes),
        compiler_params=pltpu.CompilerParams(vmem_limit_bytes=GRANT),
        cost_estimate=pl.CostEstimate(
            flops=2 * count * depth * width * side * side, bytes_accessed=2 * blocks.size, transcendentals=0
        ),
        name="output",
    )(slots, own, other, in_vmem(blocks), earlier)
    return activated, parts


def gradient_kernel(depth, width, rows, pieces, slots, hid_own, hid_other, act_own, act_other, blocks, *refs):
    out_parts, (grad_hidden, *both) = refs[:pieces], refs[pieces:]
    side = blocks.shape[-1]

    def activate(step, carry):
        at = pl.ds(pl.multiple_of(step * side, side), side)
        hidden = hid_own[:, at] + hid_other[:, at].astype(jnp.float32)
        grad_act = act_own[:, at] + act_other[:, at].astype(jnp.float32)
        grad_hidden[:, at] = (grad_act * gelu_slope(hidden)).astype(jnp.bfloat16)
        return carry

    lax.fori_loop(0, depth, activate, 0)
    for part, out_part in zip(both, out_parts):
        part[:rows] = out_part[...]
    multiply(grad_hidden, blocks, slots, depth, width, True, spread(both, rows, rows))


def gradient_product(slots, values, blocks, out_parts, depth, width):
    count = values[0].shape[0]
    side = blocks.shape[-1]
    pieces = len(out_parts)
    rows = count // pieces
    shapes = [jax.ShapeDtypeStruct((count, depth * side), jnp.bfloat16)]
    shapes += [jax.ShapeDtypeStruct((2 * rows, width * side), jnp.bfloat16)] * pieces
    grad_hidden, *both = pl.pallas_call(
        functools.partial(gradient_kernel, depth, width, rows, pieces),
        out_shape=tuple(shapes),
        in_specs=[SMEM] + [VMEM] * (5 + pieces),
        out_specs=(VMEM,) * len(shapes),
        compiler_params=pltpu.CompilerParams(vmem_limit_bytes=GRANT),
        cost_estimate=pl.CostEstimate(
            flops=2 * count * depth * width * side * side, bytes_accessed=2 * blocks.size, transcendentals=0
        ),
        name="grad_tokens",
    )(slots, *values, in_vmem(blocks), *out_parts)
    return grad_hidden, both


def outer_steps(job, begin, end, used, slots, left, right, result, turned, stage, sems):
    tall, wide, step_width = job
    count = left.shape[0]
    side = result.shape[-1]
    region = tall * wide
    buffers = stage.shape[0]
    scale = float(count) ** (-0.5)
    zero_at = stage.shape[1] - 1
    for a in range(tall):
        turned[a] = left[:, a * side : (a + 1) * side].T

    def step(index, carry):
        taken = index - begin + used
        buffer = lax.rem(taken, buffers)

        @pl.when(taken >= buffers)
        def _():
            outer_wait(job, buffer, result, stage, sems)

        at = pl.ds(pl.multiple_of(index * step_width * side, step_width * side), step_width * side)
        values = right[:, at]
        for a in range(tall):
            tile = jnp.dot(turned[a], values, preferred_element_type=jnp.float32) * scale
            tile = tile.astype(jnp.bfloat16)
            for b in range(step_width):
                place = a * step_width + b
                stage[buffer, place] = tile[:, b * side : (b + 1) * side]
                slot = slots[0, a * wide + index * step_width + b]
                pltpu.make_async_copy(
                    stage.at[buffer, jnp.where(slot >= 0, place, zero_at)],
                    result.at[jnp.where(slot >= 0, slot, slot + region)],
                    sems.at[buffer],
                ).start()
        return carry

    lax.fori_loop(begin, end, step, 0)
    return used + end - begin


def outer_wait(job, buffer, result, stage, sems):
    taken = job[0] * job[2]
    pltpu.make_async_copy(
        stage.at[buffer, pl.ds(0, taken)], result.at[pl.ds(0, taken)], sems.at[buffer]
    ).wait()


def outer_kernel(jobs, carried, *refs):
    number = len(jobs)
    operands, rest = refs[: 3 * number], refs[3 * number + 1 + carried :]
    results, (turned, stage, sems) = rest[:number], rest[number + 1 :]
    side = stage.shape[-1]
    buffers = stage.shape[0]
    for buffer in range(buffers):
        stage[buffer, stage.shape[1] - 1] = jnp.zeros((side, side), stage.dtype)
    used = 0
    for index, (job, begin, end) in enumerate(jobs):
        slots, left, right = operands[3 * index : 3 * index + 3]
        used = outer_steps(job, begin, end, used, slots, left, right, results[index], turned, stage, sems)
        following = jobs[index + 1][0] if index + 1 < number else None
        if following is None or following[0] * following[2] != job[0] * job[2]:
            for taken in range(max(0, used - buffers), used):
                outer_wait(job, taken % buffers, results[index], stage, sems)
            used = 0


def outer_job(left, right, side):
    tall, wide = left.shape[1] // side, right.shape[1] // side
    return tall, wide, next(size for size in (4, 3, 2, 1) if wide % size == 0)


def outer_product(work, side, passed, carried, name):
    jobs = [one[:3] for one in work]
    operands = [value for one in work for value in one[3:]]
    shapes = [jax.ShapeDtypeStruct((job[0] * job[1], side, side), jnp.bfloat16) for job, _, _ in jobs]
    tallest = max(job[0] for job, _, _ in jobs)
    most = max(job[0] * job[2] for job, _, _ in jobs)
    extra = [] if carried is None else [carried]
    alias = {len(operands): len(jobs)}
    if carried is not None:
        alias[len(operands) + 1] = len(jobs) - 1
    return pl.pallas_call(
        functools.partial(outer_kernel, jobs, len(extra)),
        out_shape=(*shapes, jax.ShapeDtypeStruct(passed.shape, passed.dtype)),
        in_specs=[SMEM, VMEM, VMEM] * len(jobs) + [ANY] + [HBM] * len(extra),
        out_specs=(HBM,) * len(jobs) + (ANY,),
        scratch_shapes=[
            pltpu.VMEM((tallest, side, operands[1].shape[0]), jnp.bfloat16),
            pltpu.VMEM((2, most + 1, side, side), jnp.bfloat16),
            pltpu.SemaphoreType.DMA((2,)),
        ],
        input_output_aliases=alias,
        compiler_params=pltpu.CompilerParams(vmem_limit_bytes=16 << 20),
        cost_estimate=pl.CostEstimate(
            flops=0,
            bytes_accessed=sum(2 * job[0] * job[2] * (end - begin) for job, begin, end in jobs) * side * side,
            transcendentals=0,
        ),
        name=name,
    )(*operands, passed, *extra)


def exchange(values, away, devices):
    return lax.ppermute(values, "dp", [(i, i ^ away) for i in range(devices)])


def gather(values, devices):
    if devices != 8:
        return lax.all_gather(values, "dp", axis=0, tiled=True)
    near = jnp.concatenate([values, exchange(values, 4, devices)], axis=0)
    rest = [exchange(near, away, devices) for away in (2, 3, 1)]
    return jnp.concatenate([near] + rest, axis=0)


def near_sum(parts, devices):
    total = parts[0].astype(jnp.float32)
    for part, away in zip(parts[1:], (2, 3, 1)):
        total = total + exchange(part, away, devices).astype(jnp.float32)
    return total


def far_sum(total, rows, devices):
    mine = [total[0:rows], total[2 * rows : 3 * rows]]
    theirs = jnp.concatenate([total[rows : 2 * rows], total[3 * rows :]], axis=0).astype(jnp.bfloat16)
    far = exchange(theirs, 4, devices).astype(jnp.float32)
    return [(mine[i] + far[i * rows : (i + 1) * rows]).astype(jnp.bfloat16) for i in range(2)]


def full_sum(both, rows):
    results = []
    for first in (0, rows):
        whole = jnp.concatenate([part[first : first + rows] for part in both], axis=0)
        summed = lax.psum_scatter(whole.astype(jnp.float32), "dp", scatter_dimension=0, tiled=True)
        results.append(summed.astype(jnp.bfloat16))
    return results


def swap(values, devices):
    return lax.ppermute(values, "mp", [(i, (i + 1) % devices) for i in range(devices)])


def shards(
    tokens,
    cotangent,
    inward_blocks,
    inward_rows,
    inward_cols,
    inward_count,
    outward_blocks,
    outward_rows,
    outward_cols,
    outward_count,
):
    side = inward_blocks.shape[-1]
    region = inward_blocks.shape[2]
    row_blocks = tokens.shape[1] // side
    col_blocks = region // row_blocks
    n_dp = lax.axis_size("dp")
    n_mp = lax.axis_size("mp")
    pieces = 4 if n_dp == 8 else n_dp
    inward = inward_blocks.reshape(region, side, side)
    outward = outward_blocks.reshape(region, side, side)
    in_slots, out_slots = slot_maps(
        (inward_rows, inward_cols, outward_rows, outward_cols),
        (inward_count, outward_count),
        col_blocks,
        row_blocks,
    )
    all_tokens = gather(tokens, n_dp)
    all_grads = gather(cotangent, n_dp)
    hid_own, hid_sent = first_product(
        in_slots, all_tokens, inward, in_slots, row_blocks, col_blocks, False, True, "hidden"
    )
    hid_other = swap(hid_sent, n_mp)
    act_own, act_sent = first_product(
        out_slots, all_grads, outward, hid_own, row_blocks, col_blocks, True, False, "grad_act"
    )
    act_other = swap(act_sent, n_mp)
    activated, out_parts = output_product(
        out_slots, hid_own, hid_other, outward, act_own, col_blocks, row_blocks, pieces
    )
    grad_hidden, both = gradient_product(
        in_slots, (hid_own, hid_other, act_own, act_other), inward, out_parts, col_blocks, row_blocks
    )
    rows = tokens.shape[0]
    out_job = outer_job(activated, all_grads, side)
    in_job = outer_job(all_tokens, grad_hidden, side)
    in_steps = in_job[1] // in_job[2]
    begun = in_steps // 3
    work = [(out_job, 0, out_job[1] // out_job[2], out_slots, activated, all_grads)]
    if begun:
        work.append((in_job, 0, begun, in_slots, all_tokens, grad_hidden))
    grad_outward, *started, own = outer_product(work, side, both[0], None, "outward")
    both = [own, *both[1:]]
    nearly = near_sum(both, n_dp) if n_dp == 8 else own
    work = [(in_job, begun, in_steps, in_slots, all_tokens, grad_hidden)]
    grad_inward, _ = outer_product(work, side, nearly[0:8, 0:128], started[0] if begun else None, "inward")
    out_tokens, grad_tokens = far_sum(nearly, rows, n_dp) if n_dp == 8 else full_sum(both, rows)
    return (
        out_tokens,
        grad_tokens,
        grad_inward.reshape(inward_blocks.shape),
        grad_outward.reshape(outward_blocks.shape),
    )


def solution(mesh):
    in_specs = (
        P(("sweep", "dp"), "mp"),
        P(("sweep", "dp"), "mp"),
        P(("sweep", "mp"), "dp", None, None, None),
        P(("sweep", "mp"), "dp", None),
        P(("sweep", "mp"), "dp", None),
        P(("sweep", "mp"), "dp"),
        P(("sweep", "dp"), "mp", None, None, None),
        P(("sweep", "dp"), "mp", None),
        P(("sweep", "dp"), "mp", None),
        P(("sweep", "dp"), "mp"),
    )
    out_specs = (
        P(("sweep", "dp"), "mp"),
        P(("sweep", "dp"), "mp"),
        P(("sweep", "mp"), "dp", None, None, None),
        P(("sweep", "dp"), "mp", None, None, None),
    )
    return jax.shard_map(shards, mesh=mesh, in_specs=in_specs, out_specs=out_specs, check_vma=False)
```

time: 75.5 us -> 72.6 us (0.962)
  Pallas kernels: 47.7 us -> 45.1 us
    pallas_call x4 -> x3, Pallas kernels: 19.7 us -> 16.7 us  [the longest x2 15.2 us: outer_product(): pl.pallas_call(functools.partial(outer_kernel, jobs, len(extra)), out_sha...]
  transfers between devices with their start and end apart: 14 -> 14, of which waited for: 2 -> 2; matrix products, arithmetic and copies ran while one was open for 3% -> 3% of each run, Pallas kernels for 53% -> 52%
where the time goes in v2:
time: 72.6 us; the launch traced here: 72.3 us
  Pallas kernels  45.1 us (62%)
  starting transfers between devices  18.8 us (26%)
  waiting for transfers between devices  2.96 us (4%)
  local copies, waits for them, and re-layouts  2.46 us (3%)
  between operations  2.23 us (3%)
  other arithmetic  0.8 us (1%)
    ppermute x12, starting transfers between devices, exchange(): return lax.ppermute(values, 'dp', [(i, i ^ away) for i in range(devices)])  18.2 us
    pallas_call x2, Pallas kernels, outer_product(): pl.pallas_call(functools.partial(outer_kernel, jobs, len(extra)), out_sha...  15.2 us
    pallas_call x2, Pallas kernels, first_product(): pl.pallas_call(functools.partial(first_kernel, depth, width, across), out...  14.8 us
    pallas_call x1, Pallas kernels, gradient_product(): pl.pallas_call(functools.partial(gradient_kernel, depth, width, rows, pie...  7.7 us
    pallas_call x1, Pallas kernels, output_product(): pl.pallas_call(functools.partial(output_kernel, depth, width, rows), out_...  5.91 us
    ppermute x12, waiting for transfers between devices, exchange(): return lax.ppermute(values, 'dp', [(i, i ^ away) for i in range(devices)])  2.96 us
    unnamed x18, local copies, waits for them, and re-layouts  2.42 us
    pallas_call x1, Pallas kernels, slot_maps(): pl.pallas_call(functools.partial(slots_kernel, (in_width, out_width)), ou...  1.54 us
  transfers between devices with their start and end apart: 14, of which 2 were waited for; matrix products, arithmetic and copies ran while one was open for 3% of the time, Pallas kernels for 52%

profile of v2, /device:TPU:0, one launch (start us, length us, event | category | flops | bytes accessed | tf_op | source)
XLA Modules:
  0.0 72.3 jit_solution(14392118996769978303)
XLA Ops:
  0.6 4.1 %collective-permute-start = (bf16[8,3072]{1,0:T(8,128)(2,1)}, bf16[8,3072]{1,0:T(8,128)(2,1)S(1)}, u32[]{:S(2)}, u32[]{:S(2)}) collective-permute-start(bf16[8,3072]{1,0:T(8,128)(2,1)} %param.10), channel_id=1, source_target_pairs={{0,8},{2,10},{4,12},{6,14},{8,0},{10,2},{12,4},{14,6},{1,9},{3,11}... | collective-permute-start | bytes 147464 | tf_op jit(solution)/shard_map/ppermute | solution.py:394
  4.7 0.1 collective-permute-start.5
  4.8 1.6 %constant_dynamic-update-slice_fusion.1 = (bf16[16,3072]{1,0:T(8,128)(2,1)S(1)}, bf16[64,3072]{1,0:T(8,128)(2,1)S(1)}) fusion(bf16[8,3072]{1,0:T(8,128)(2,1)} %param.10), kind=kLoop, calls=%fused_computation.7 | loop fusion | bytes 147456
  6.4 0.8 %constant_dynamic-update-slice_fusion.8 = (bf16[16,3072]{1,0:T(8,128)(2,1)S(1)}, bf16[64,3072]{1,0:T(8,128)(2,1)S(1)}) fusion(bf16[8,3072]{1,0:T(8,128)(2,1)} %param.11), kind=kLoop, calls=%fused_computation.14 | loop fusion | bytes 147456
  8.5 1.5 %slot_maps.1 = (s32[1,576]{1,0:T(1,128)S(1)}, s32[1,576]{1,0:T(1,128)S(1)}) custom-call(s32[1,1,576]{2,1,0:T(1,128)} %refs_0_.1, s32[1,1,576]{2,1,0:T(1,128)} %refs_1_.1, s32[1,1,576]{2,1,0:T(1,128)} %refs_2_.1, s32[1,1,576]{2,1,0:T(1,128)} %refs_3_.1, s32[1,1]{1,0:T(1,128)S(6)} %copy.30.refs_4_, s32[1,1]{1,0:T(1,128)S(6)} %copy.31.refs_5_), custom_call_target="tpu_custom_call" | custom-call | bytes 4194304 | tf_op jit(solution)/shard_map/slot_maps/pallas_call | solution.py:63
  10.0 2.2 %collective-permute-start.1 = (bf16[16,3072]{1,0:T(8,128)(2,1)S(1)}, bf16[16,3072]{1,0:T(8,128)(2,1)S(1)}, u32[]{:S(2)}, u32[]{:S(2)}) collective-permute-start(bf16[16,3072]{1,0:T(8,128)(2,1)S(1)} %get-tuple-element.54), channel_id=1, source_target_pairs={{0,4},{2,6},{4,0},{6,2},{8,12},{10,14},{12,8},{14,10},{1,5},{3,7},... | collective-permute-start | bytes 294920 | tf_op jit(solution)/shard_map/ppermute | solution.py:394
  12.3 1.4 %collective-permute-start.2 = (bf16[16,3072]{1,0:T(8,128)(2,1)S(1)}, bf16[16,3072]{1,0:T(8,128)(2,1)S(1)}, u32[]{:S(2)}, u32[]{:S(2)}) collective-permute-start(bf16[16,3072]{1,0:T(8,128)(2,1)S(1)} %get-tuple-element.54), channel_id=1, source_target_pairs={{0,6},{2,4},{4,2},{6,0},{8,14},{10,12},{12,10},{14,8},{1,7},{3,5},... | collective-permute-start | bytes 294920 | tf_op jit(solution)/shard_map/ppermute | solution.py:394
  13.6 0.2 collective-permute-start.3
  13.8 2.0 %collective-permute-start.6 = (bf16[16,3072]{1,0:T(8,128)(2,1)S(1)}, bf16[16,3072]{1,0:T(8,128)(2,1)S(1)}, u32[]{:S(2)}, u32[]{:S(2)}) collective-permute-start(bf16[16,3072]{1,0:T(8,128)(2,1)S(1)} %get-tuple-element.50), channel_id=1, source_target_pairs={{0,4},{2,6},{4,0},{6,2},{8,12},{10,14},{12,8},{14,10},{1,5},{3,7},... | collective-permute-start | bytes 294920 | tf_op jit(solution)/shard_map/ppermute | solution.py:394
  15.8 1.4 %collective-permute-start.7 = (bf16[16,3072]{1,0:T(8,128)(2,1)S(1)}, bf16[16,3072]{1,0:T(8,128)(2,1)S(1)}, u32[]{:S(2)}, u32[]{:S(2)}) collective-permute-start(bf16[16,3072]{1,0:T(8,128)(2,1)S(1)} %get-tuple-element.50), channel_id=1, source_target_pairs={{0,6},{2,4},{4,2},{6,0},{8,14},{10,12},{12,10},{14,8},{1,7},{3,5},... | collective-permute-start | bytes 294920 | tf_op jit(solution)/shard_map/ppermute | solution.py:394
  17.2 0.0 collective-permute-done.1
  17.2 0.6 collective-permute-start.8
  17.9 1.6 %collective-permute-done.2 = bf16[16,3072]{1,0:T(8,128)(2,1)S(1)} collective-permute-done((bf16[16,3072]{1,0:T(8,128)(2,1)S(1)}, bf16[16,3072]{1,0:T(8,128)(2,1)S(1)}, u32[]{:S(2)}, u32[]{:S(2)}) %collective-permute-start.2) | collective-permute-done | bytes 98336 | tf_op jit(solution)/shard_map/ppermute | solution.py:394
  19.5 1.3 %collective-permute-done.3 = bf16[16,3072]{1,0:T(8,128)(2,1)S(1)} collective-permute-done((bf16[16,3072]{1,0:T(8,128)(2,1)S(1)}, bf16[16,3072]{1,0:T(8,128)(2,1)S(1)}, u32[]{:S(2)}, u32[]{:S(2)}) %collective-permute-start.3) | collective-permute-done | bytes 98336 | tf_op jit(solution)/shard_map/ppermute | solution.py:394
  20.8 7.8 %hidden.1 = (f32[64,3072]{1,0:T(8,128)S(1)}, bf16[64,3072]{1,0:T(8,128)(2,1)S(1)}) custom-call(s32[1,576]{1,0:T(1,128)S(1)} %get-tuple-element.25.slots.earlier.refs_3_.refs_0_, bf16[64,3072]{1,0:T(8,128)(2,1)S(1)} %constant_dynamic-update-slice_fusion.2.lhs.refs_4_.refs_1_, bf16[576,128,128]{2,1,0:T(8,128)(2,1)} %bitcast.6, ...), custom_call_target="tpu_custom_call" | custom-call | flops 1207959552 | bytes 18874368 | tf_op jit(solution)/shard_map/hidden/pallas_call | solution.py:190
  28.6 0.1 collective-permute-start.4
  28.7 0.0 collective-permute-done.6
  28.8 0.0 slice-start
  28.8 0.0 slice-start.1
  28.8 0.0 slice-start.2
  28.8 7.0 %grad_act.1 = (f32[64,3072]{1,0:T(8,128)S(1)}, bf16[64,3072]{1,0:T(8,128)(2,1)S(1)}) custom-call(s32[1,576]{1,0:T(1,128)S(1)} %get-tuple-element.24.slots.refs_0_, bf16[64,3072]{1,0:T(8,128)(2,1)S(1)} %constant_dynamic-update-slice_fusion.9.lhs.refs_2_, bf16[576,128,128]{2,1,0:T(8,128)(2,1)S(1)} %bitcast.4, f32[64,3072]{1,0:T(8,128)S(1)} %get-tuple-element.26.earlier.own.hid_own), custom_call_target="tpu_custom_call" | custom-call | flops 1207959552 | bytes 18874368 | tf_op jit(solution)/shard_map/grad_act/pallas_call | solution.py:190
  35.8 0.6 collective-permute-start.9
  36.4 5.9 %output.1 = (bf16[64,3072]{1,0:T(8,128)(2,1)S(1)}, bf16[16,3072]{1,0:T(8,128)(2,1)S(1)}, bf16[16,3072]{1,0:T(8,128)(2,1)S(1)}, bf16[16,3072]{1,0:T(8,128)(2,1)S(1)}, bf16[16,3072]{1,0:T(8,128)(2,1)S(1)}) custom-call(s32[1,576]{1,0:T(1,128)S(1)} %get-tuple-element.24.slots.refs_0_, f32[64,3072]{1,0:T(8,128)S(1)} %get-tuple-element.26.earlier.own.hid_own, ...), custom_call_target="tpu_custom_call" | custom-call | flops 1207959552 | bytes 18874368 | tf_op jit(solution)/shard_map/output/pallas_call | solution.py:240
  42.3 7.7 %grad_tokens.1 = (bf16[64,3072]{1,0:T(8,128)(2,1)S(1)}, bf16[32,3072]{1,0:T(8,128)(2,1)S(1)}, bf16[32,3072]{1,0:T(8,128)(2,1)S(1)}, bf16[32,3072]{1,0:T(8,128)(2,1)S(1)}, bf16[32,3072]{1,0:T(8,128)(2,1)S(1)}) custom-call(s32[1,576]{1,0:T(1,128)S(1)} %get-tuple-element.25.slots.earlier.refs_3_.refs_0_, f32[64,3072]{1,0:T(8,128)S(1)} %get-tuple-element.26.earlier.own.hid_own, ...), custom_call_target="tpu_custom_call" | custom-call | flops 1207959552 | bytes 18874368 | tf_op jit(solution)/shard_map/grad_tokens/pallas_call | solution.py:278
  50.0 0.7 %collective-permute-start.12 = (bf16[32,3072]{1,0:T(8,128)(2,1)S(1)}, bf16[32,3072]{1,0:T(8,128)(2,1)S(1)}, u32[]{:S(2)}, u32[]{:S(2)}) collective-permute-start(bf16[32,3072]{1,0:T(8,128)(2,1)S(1)} %get-tuple-element.40), channel_id=1, source_target_pairs={{0,2},{2,0},{4,6},{6,4},{8,10},{10,8},{12,14},{14,12},{1,3},{3,1},... | collective-permute-start | bytes 589832 | tf_op jit(solution)/shard_map/ppermute | solution.py:394
  50.8 2.6 %collective-permute-start.11 = (bf16[32,3072]{1,0:T(8,128)(2,1)S(1)}, bf16[32,3072]{1,0:T(8,128)(2,1)S(1)}, u32[]{:S(2)}, u32[]{:S(2)}) collective-permute-start(bf16[32,3072]{1,0:T(8,128)(2,1)S(1)} %get-tuple-element.39), channel_id=1, source_target_pairs={{0,6},{2,4},{4,2},{6,0},{8,14},{10,12},{12,10},{14,8},{1,7},{3,5},... | collective-permute-start | bytes 589832 | tf_op jit(solution)/shard_map/ppermute | solution.py:394
  53.4 0.2 collective-permute-start.10
  53.6 9.7 %outward.1 = (bf16[576,128,128]{2,1,0:T(8,128)(2,1)}, bf16[576,128,128]{2,1,0:T(8,128)(2,1)}, bf16[32,3072]{1,0:T(8,128)(2,1)S(1)}) custom-call(s32[1,576]{1,0:T(1,128)S(1)} %get-tuple-element.24.slots.refs_0_, bf16[64,3072]{1,0:T(8,128)(2,1)S(1)} %get-tuple-element.29.refs_1_, ...), custom_call_target="tpu_custom_call", output_to_operand_aliasing={{2}: (6, {})} | custom-call | bytes 25165824 | tf_op jit(solution)/shard_map/outward/pallas_call | solution.py:372
  63.3 0.1 fusion.2
  63.5 2.7 %collective-permute-start.13 = (bf16[16,3072]{1,0:T(8,128)(2,1)S(1)}, bf16[16,3072]{1,0:T(8,128)(2,1)S(1)}, u32[]{:S(2)}, u32[]{:S(2)}) collective-permute-start(bf16[16,3072]{1,0:T(8,128)(2,1)S(1)} %pad_maximum_fusion), channel_id=1, source_target_pairs={{0,8},{2,10},{4,12},{6,14},{8,0},{10,2},{12,4},{14,6},{1,9},{3,11}... | collective-permute-start | bytes 294920 | tf_op jit(solution)/shard_map/ppermute | solution.py:394
  66.1 5.5 %inward.1 = (bf16[576,128,128]{2,1,0:T(8,128)(2,1)}, f32[8,128]{1,0:T(8,128)S(1)}) custom-call(s32[1,576]{1,0:T(1,128)S(1)} %get-tuple-element.25.slots.earlier.refs_3_.refs_0_, bf16[64,3072]{1,0:T(8,128)(2,1)S(1)} %constant_dynamic-update-slice_fusion.2.lhs.refs_4_.refs_1_, ...), custom_call_target="tpu_custom_call", output_to_operand_aliasing={{1}: (3, {}), {0}: (4, {})} | custom-call | bytes 12582912 | tf_op jit(solution)/shard_map/inward/pallas_call | solution.py:372
  71.7 0.7 fusion
  (32 shorter events, 0.1 us)
Async XLA Ops:
  0.6 28.1 %copy-start = (bf16[1,1,576,128,128]{4,3,2,1,0:T(8,128)(2,1)S(1)}, bf16[1,1,576,128,128]{4,3,2,1,0:T(8,128)(2,1)}, u32[]{:S(2)}) copy-start(bf16[1,1,576,128,128]{4,3,2,1,0:T(8,128)(2,1)} %param.16) | copy-start | bytes 56623108
  0.6 9.4 %collective-permute-start = (bf16[8,3072]{1,0:T(8,128)(2,1)}, bf16[8,3072]{1,0:T(8,128)(2,1)S(1)}, u32[]{:S(2)}, u32[]{:S(2)}) collective-permute-start(bf16[8,3072]{1,0:T(8,128)(2,1)} %param.10), channel_id=1, source_target_pairs={{0,8},{2,10},{4,12},{6,14},{8,0},{10,2},{12,4},{14,6},{1,9},{3,11}... | collective-permute-start | bytes 147464 | tf_op jit(solution)/shard_map/ppermute | solution.py:394
  4.7 9.1 %collective-permute-start.5 = (bf16[8,3072]{1,0:T(8,128)(2,1)}, bf16[8,3072]{1,0:T(8,128)(2,1)S(1)}, u32[]{:S(2)}, u32[]{:S(2)}) collective-permute-start(bf16[8,3072]{1,0:T(8,128)(2,1)} %param.11), channel_id=1, source_target_pairs={{0,8},{2,10},{4,12},{6,14},{8,0},{10,2},{12,4},{14,6},{1,9},{3,11}... | collective-permute-start | bytes 147464 | tf_op jit(solution)/shard_map/ppermute | solution.py:394
  10.0 7.2 %collective-permute-start.1 = (bf16[16,3072]{1,0:T(8,128)(2,1)S(1)}, bf16[16,3072]{1,0:T(8,128)(2,1)S(1)}, u32[]{:S(2)}, u32[]{:S(2)}) collective-permute-start(bf16[16,3072]{1,0:T(8,128)(2,1)S(1)} %get-tuple-element.54), channel_id=1, source_target_pairs={{0,4},{2,6},{4,0},{6,2},{8,12},{10,14},{12,8},{14,10},{1,5},{3,7},... | collective-permute-start | bytes 294920 | tf_op jit(solution)/shard_map/ppermute | solution.py:394
  12.3 7.2 %collective-permute-start.2 = (bf16[16,3072]{1,0:T(8,128)(2,1)S(1)}, bf16[16,3072]{1,0:T(8,128)(2,1)S(1)}, u32[]{:S(2)}, u32[]{:S(2)}) collective-permute-start(bf16[16,3072]{1,0:T(8,128)(2,1)S(1)} %get-tuple-element.54), channel_id=1, source_target_pairs={{0,6},{2,4},{4,2},{6,0},{8,14},{10,12},{12,10},{14,8},{1,7},{3,5},... | collective-permute-start | bytes 294920 | tf_op jit(solution)/shard_map/ppermute | solution.py:394
  13.6 7.2 %collective-permute-start.3 = (bf16[16,3072]{1,0:T(8,128)(2,1)S(1)}, bf16[16,3072]{1,0:T(8,128)(2,1)S(1)}, u32[]{:S(2)}, u32[]{:S(2)}) collective-permute-start(bf16[16,3072]{1,0:T(8,128)(2,1)S(1)} %get-tuple-element.54), channel_id=1, source_target_pairs={{0,2},{2,0},{4,6},{6,4},{8,10},{10,8},{12,14},{14,12},{1,3},{3,1},... | collective-permute-start | bytes 294920 | tf_op jit(solution)/shard_map/ppermute | solution.py:394
  13.8 14.9 %collective-permute-start.6 = (bf16[16,3072]{1,0:T(8,128)(2,1)S(1)}, bf16[16,3072]{1,0:T(8,128)(2,1)S(1)}, u32[]{:S(2)}, u32[]{:S(2)}) collective-permute-start(bf16[16,3072]{1,0:T(8,128)(2,1)S(1)} %get-tuple-element.50), channel_id=1, source_target_pairs={{0,4},{2,6},{4,0},{6,2},{8,12},{10,14},{12,8},{14,10},{1,5},{3,7},... | collective-permute-start | bytes 294920 | tf_op jit(solution)/shard_map/ppermute | solution.py:394
  15.8 12.9 %collective-permute-start.7 = (bf16[16,3072]{1,0:T(8,128)(2,1)S(1)}, bf16[16,3072]{1,0:T(8,128)(2,1)S(1)}, u32[]{:S(2)}, u32[]{:S(2)}) collective-permute-start(bf16[16,3072]{1,0:T(8,128)(2,1)S(1)} %get-tuple-element.50), channel_id=1, source_target_pairs={{0,6},{2,4},{4,2},{6,0},{8,14},{10,12},{12,10},{14,8},{1,7},{3,5},... | collective-permute-start | bytes 294920 | tf_op jit(solution)/shard_map/ppermute | solution.py:394
  17.2 11.5 %collective-permute-start.8 = (bf16[16,3072]{1,0:T(8,128)(2,1)S(1)}, bf16[16,3072]{1,0:T(8,128)(2,1)S(1)}, u32[]{:S(2)}, u32[]{:S(2)}) collective-permute-start(bf16[16,3072]{1,0:T(8,128)(2,1)S(1)} %get-tuple-element.50), channel_id=1, source_target_pairs={{0,2},{2,0},{4,6},{6,4},{8,10},{10,8},{12,14},{14,12},{1,3},{3,1},... | collective-permute-start | bytes 294920 | tf_op jit(solution)/shard_map/ppermute | solution.py:394
  28.6 7.8 %collective-permute-start.4 = (bf16[64,3072]{1,0:T(8,128)(2,1)S(1)}, bf16[64,3072]{1,0:T(8,128)(2,1)S(1)}, u32[]{:S(2)}, u32[]{:S(2)}) collective-permute-start(bf16[64,3072]{1,0:T(8,128)(2,1)S(1)} %get-tuple-element.27), channel_id=1, source_target_pairs={{0,1},{1,0},{2,3},{3,2},{4,5},{5,4},{6,7},{7,6},{8,9},{9,8},{10,11... | collective-permute-start | bytes 1179656 | tf_op jit(solution)/shard_map/ppermute | solution.py:429
  28.8 13.5 %slice-start = ((s8[18874368]{0:T(1024)(128)(4,1)}), s8[4194304]{0:T(1024)(128)(4,1)S(1)}, s32[]{:S(2)}) async-start(s8[18874368]{0:T(1024)(128)(4,1)} %bitcast.7), calls=%async_computation | async-start | bytes 8388608
  28.8 13.5 %slice-start.1 = ((s8[18874368]{0:T(1024)(128)(4,1)}), s8[4194304]{0:T(1024)(128)(4,1)S(1)}, s32[]{:S(2)}) async-start(s8[18874368]{0:T(1024)(128)(4,1)} %bitcast.7), calls=%async_computation.1 | async-start | bytes 8388608
  28.8 13.5 %slice-start.2 = ((s8[18874368]{0:T(1024)(128)(4,1)}), s8[4194304]{0:T(1024)(128)(4,1)S(1)}, s32[]{:S(2)}) async-start(s8[18874368]{0:T(1024)(128)(4,1)} %bitcast.7), calls=%async_computation.2 | async-start | bytes 8388608
  35.8 6.5 %collective-permute-start.9 = (bf16[64,3072]{1,0:T(8,128)(2,1)S(1)}, bf16[64,3072]{1,0:T(8,128)(2,1)S(1)}, u32[]{:S(2)}, u32[]{:S(2)}) collective-permute-start(bf16[64,3072]{1,0:T(8,128)(2,1)S(1)} %get-tuple-element.30), channel_id=1, source_target_pairs={{0,1},{1,0},{2,3},{3,2},{4,5},{5,4},{6,7},{7,6},{8,9},{9,8},{10,11... | collective-permute-start | bytes 1179656 | tf_op jit(solution)/shard_map/ppermute | solution.py:429
  36.4 6.0 %slice-start.3 = ((s8[18874368]{0:T(1024)(128)(4,1)}), s8[4194304]{0:T(1024)(128)(4,1)S(1)}, s32[]{:S(2)}) async-start(s8[18874368]{0:T(1024)(128)(4,1)} %bitcast.7), calls=%async_computation.3 | async-start | bytes 8388608
  36.4 6.0 %slice-start.4 = ((s8[18874368]{0:T(1024)(128)(4,1)}), s8[2097152]{0:T(1024)(128)(4,1)S(1)}, s32[]{:S(2)}) async-start(s8[18874368]{0:T(1024)(128)(4,1)} %bitcast.7), calls=%async_computation.4 | async-start | bytes 4194304
  50.0 13.3 %collective-permute-start.12 = (bf16[32,3072]{1,0:T(8,128)(2,1)S(1)}, bf16[32,3072]{1,0:T(8,128)(2,1)S(1)}, u32[]{:S(2)}, u32[]{:S(2)}) collective-permute-start(bf16[32,3072]{1,0:T(8,128)(2,1)S(1)} %get-tuple-element.40), channel_id=1, source_target_pairs={{0,2},{2,0},{4,6},{6,4},{8,10},{10,8},{12,14},{14,12},{1,3},{3,1},... | collective-permute-start | bytes 589832 | tf_op jit(solution)/shard_map/ppermute | solution.py:394
  50.8 12.5 %collective-permute-start.11 = (bf16[32,3072]{1,0:T(8,128)(2,1)S(1)}, bf16[32,3072]{1,0:T(8,128)(2,1)S(1)}, u32[]{:S(2)}, u32[]{:S(2)}) collective-permute-start(bf16[32,3072]{1,0:T(8,128)(2,1)S(1)} %get-tuple-element.39), channel_id=1, source_target_pairs={{0,6},{2,4},{4,2},{6,0},{8,14},{10,12},{12,10},{14,8},{1,7},{3,5},... | collective-permute-start | bytes 589832 | tf_op jit(solution)/shard_map/ppermute | solution.py:394
  53.4 10.0 %collective-permute-start.10 = (bf16[32,3072]{1,0:T(8,128)(2,1)S(1)}, bf16[32,3072]{1,0:T(8,128)(2,1)S(1)}, u32[]{:S(2)}, u32[]{:S(2)}) collective-permute-start(bf16[32,3072]{1,0:T(8,128)(2,1)S(1)} %get-tuple-element.38), channel_id=1, source_target_pairs={{0,4},{2,6},{4,0},{6,2},{8,12},{10,14},{12,8},{14,10},{1,5},{3,7},... | collective-permute-start | bytes 589832 | tf_op jit(solution)/shard_map/ppermute | solution.py:394
  63.5 8.1 %collective-permute-start.13 = (bf16[16,3072]{1,0:T(8,128)(2,1)S(1)}, bf16[16,3072]{1,0:T(8,128)(2,1)S(1)}, u32[]{:S(2)}, u32[]{:S(2)}) collective-permute-start(bf16[16,3072]{1,0:T(8,128)(2,1)S(1)} %pad_maximum_fusion), channel_id=1, source_target_pairs={{0,8},{2,10},{4,12},{6,14},{8,0},{10,2},{12,4},{14,6},{1,9},{3,11}... | collective-permute-start | bytes 294920 | tf_op jit(solution)/shard_map/ppermute | solution.py:394

commit v3 on v2

--- a/solution.py
+++ b/solution.py
@@ -29,7 +29,7 @@
 
 
 def slots_kernel(widths, *refs):
-    far, counts, slots, near, (spread_out, sems) = refs[:4], refs[4:6], refs[6:8], refs[8:12], refs[12:]
+    far, counts, slots, near, (spread_out, sems) = refs[:4], refs[4:6], refs[7:9], refs[9:13], refs[13:]
     copies = [pltpu.make_async_copy(*ends, sems.at[index]) for index, ends in enumerate(zip(far, near))]
     for copy in copies:
         copy.start()
@@ -55,7 +55,7 @@
         slots[which][...] = total[:, 0:region]
 
 
-def slot_maps(places, counts, in_width, out_width):
+def slot_maps(places, counts, earlier, in_width, out_width):
     region = places[0].shape[-1]
     lanes = -(-region // 128) * 128
     shape = jax.ShapeDtypeStruct((1, region), jnp.int32)
@@ -63,13 +63,13 @@
     return pl.pallas_call(
         functools.partial(slots_kernel, (in_width, out_width)),
         out_shape=(shape, shape),
-        in_specs=[HBM] * 4 + [SMEM] * 2,
+        in_specs=[HBM] * 4 + [SMEM] * 2 + [ANY],
         out_specs=(VMEM, VMEM),
         scratch_shapes=near + [pltpu.VMEM((8, lanes), jnp.int32), pltpu.SemaphoreType.DMA((4,))],
         compiler_params=pltpu.CompilerParams(vmem_limit_bytes=GRANT),
         cost_estimate=pl.CostEstimate(flops=0, bytes_accessed=4 << 20, transcendentals=0),
         name="slot_maps",
-    )(*[in_hbm(place) for place in places], *counts)
+    )(*[in_hbm(place) for place in places], *counts, earlier)
 
 
 def pair(count):
@@ -166,18 +166,24 @@
         column(step, step % buffers)
 
 
-def first_kernel(depth, width, across, slots, lhs, blocks, earlier, own, sent, *fetch):
+def first_kernel(depth, width, across, pieces, slots, *refs):
+    parts, (blocks, earlier, whole, own, sent, *fetch) = refs[:pieces], refs[pieces:]
+    rows = whole.shape[0] // pieces
+    for index, part in enumerate(parts):
+        whole[index * rows : (index + 1) * rows] = part[...]
+
     def store(start, size, total):
         own[:, pl.ds(start, size)] = total
         sent[:, pl.ds(start, size)] = total.astype(jnp.bfloat16)
 
     run = stream if fetch else multiply
-    run(lhs, blocks, slots, depth, width, across, store, *fetch)
-
-
-def first_product(slots, lhs, blocks, earlier, depth, width, across, streamed, name):
+    run(whole, blocks, slots, depth, width, across, store, *fetch)
+
+
+def first_product(slots, parts, blocks, earlier, depth, width, across, streamed, name):
     side = blocks.shape[-1]
-    shape = (lhs.shape[0], width * side)
+    count = sum(part.shape[0] for part in parts)
+    shape = (count, width * side)
     scratch, grant = [], GRANT
     if streamed:
         wide = next(size for size in (4, 3, 2, 1) if width % size == 0)
@@ -188,17 +194,21 @@
         ]
         grant = 16 << 20
     return pl.pallas_call(
-        functools.partial(first_kernel, depth, width, across),
-        out_shape=(jax.ShapeDtypeStruct(shape, jnp.float32), jax.ShapeDtypeStruct(shape, jnp.bfloat16)),
-        in_specs=[SMEM, VMEM, HBM if streamed else VMEM, ANY],
-        out_specs=(VMEM, VMEM),
+        functools.partial(first_kernel, depth, width, across, len(parts)),
+        out_shape=(
+            jax.ShapeDtypeStruct((count, depth * side), jnp.bfloat16),
+            jax.ShapeDtypeStruct(shape, jnp.float32),
+            jax.ShapeDtypeStruct(shape, jnp.bfloat16),
+        ),
+        in_specs=[SMEM] + [VMEM] * len(parts) + [HBM if streamed else VMEM, ANY],
+        out_specs=(VMEM, VMEM, VMEM),
         scratch_shapes=scratch,
         compiler_params=pltpu.CompilerParams(vmem_limit_bytes=grant),
         cost_estimate=pl.CostEstimate(
-            flops=2 * lhs.size * width * side, bytes_accessed=2 * blocks.size, transcendentals=0
+            flops=2 * count * depth * width * side * side, bytes_accessed=2 * blocks.size, transcendentals=0
         ),
         name=name,
-    )(slots, lhs, in_hbm(blocks) if streamed else in_vmem(blocks), earlier)
+    )(slots, *parts, in_hbm(blocks) if streamed else in_vmem(blocks), earlier)
 
 
 def in_hbm(values):
@@ -396,10 +406,9 @@
 
 def gather(values, devices):
     if devices != 8:
-        return lax.all_gather(values, "dp", axis=0, tiled=True)
+        return [lax.all_gather(values, "dp", axis=0, tiled=True)]
     near = jnp.concatenate([values, exchange(values, 4, devices)], axis=0)
-    rest = [exchange(near, away, devices) for away in (2, 3, 1)]
-    return jnp.concatenate([near] + rest, axis=0)
+    return [near] + [exchange(near, away, devices) for away in (2, 3, 1)]
 
 
 def near_sum(parts, devices):
@@ -450,20 +459,21 @@
     pieces = 4 if n_dp == 8 else n_dp
     inward = inward_blocks.reshape(region, side, side)
     outward = outward_blocks.reshape(region, side, side)
+    token_parts = gather(tokens, n_dp)
+    grad_parts = gather(cotangent, n_dp)
     in_slots, out_slots = slot_maps(
         (inward_rows, inward_cols, outward_rows, outward_cols),
         (inward_count, outward_count),
+        token_parts[0],
         col_blocks,
         row_blocks,
     )
-    all_tokens = gather(tokens, n_dp)
-    all_grads = gather(cotangent, n_dp)
-    hid_own, hid_sent = first_product(
-        in_slots, all_tokens, inward, in_slots, row_blocks, col_blocks, False, True, "hidden"
+    all_tokens, hid_own, hid_sent = first_product(
+        in_slots, token_parts, inward, in_slots, row_blocks, col_blocks, False, True, "hidden"
     )
     hid_other = swap(hid_sent, n_mp)
-    act_own, act_sent = first_product(
-        out_slots, all_grads, outward, hid_own, row_blocks, col_blocks, True, False, "grad_act"
+    all_grads, act_own, act_sent = first_product(
+        out_slots, grad_parts, outward, hid_own, row_blocks, col_blocks, True, False, "grad_act"
     )
     act_other = swap(act_sent, n_mp)
     activated, out_parts = output_product(

time: 72.6 us -> 69.6 us (0.959)
  waiting for transfers between devices: 2.96 us -> 0.49 us
    ppermute x12, waiting for transfers between devices: 2.96 us -> 0.48 us  [exchange(): return lax.ppermute(values, 'dp', [(i, i ^ away) for i in range(devices)])]
    unnamed x18 -> x14, local copies, waits for them, and re-layouts: 2.42 us -> 2.38 us
  transfers between devices with their start and end apart: 14 -> 14, of which waited for: 2 -> 1; matrix products, arithmetic and copies ran while one was open for 3% -> 3% of each run, Pallas kernels for 52% -> 54%
where the time goes in v3:
time: 69.6 us; the launch traced here: 69.3 us
  Pallas kernels  45 us (65%)
  starting transfers between devices  18.4 us (26%)
  local copies, waits for them, and re-layouts  2.4 us (3%)
  between operations  2.21 us (3%)
  other arithmetic  0.79 us (1%)
    ppermute x12, starting transfers between devices, exchange(): return lax.ppermute(values, 'dp', [(i, i ^ away) for i in range(devices)])  17.8 us
    pallas_call x2, Pallas kernels, outer_product(): pl.pallas_call(functools.partial(outer_kernel, jobs, len(extra)), out_sha...  15.2 us
    pallas_call x2, Pallas kernels, first_product(): pl.pallas_call(functools.partial(first_kernel, depth, width, across, len(...  14.8 us
    pallas_call x1, Pallas kernels, gradient_product(): pl.pallas_call(functools.partial(gradient_kernel, depth, width, rows, pie...  7.7 us
    pallas_call x1, Pallas kernels, output_product(): pl.pallas_call(functools.partial(output_kernel, depth, width, rows), out_...  5.82 us
    unnamed x14, local copies, waits for them, and re-layouts  2.38 us
    pallas_call x1, Pallas kernels, slot_maps(): pl.pallas_call(functools.partial(slots_kernel, (in_width, out_width)), ou...  1.53 us
  transfers between devices with their start and end apart: 14, of which 1 were waited for; matrix products, arithmetic and copies ran while one was open for 3% of the time, Pallas kernels for 54%

profile of v3, /device:TPU:0, one launch (start us, length us, event | category | flops | bytes accessed | tf_op | source)
XLA Modules:
  0.0 69.3 jit_solution(2237933736910501874)
XLA Ops:
  0.6 4.1 %collective-permute-start = (bf16[8,3072]{1,0:T(8,128)(2,1)}, bf16[8,3072]{1,0:T(8,128)(2,1)S(1)}, u32[]{:S(2)}, u32[]{:S(2)}) collective-permute-start(bf16[8,3072]{1,0:T(8,128)(2,1)} %param.10), channel_id=1, source_target_pairs={{0,8},{2,10},{4,12},{6,14},{8,0},{10,2},{12,4},{14,6},{1,9},{3,11}... | collective-permute-start | bytes 147464 | tf_op jit(solution)/shard_map/ppermute | solution.py:404
  4.7 0.1 collective-permute-start.5
  4.8 1.5 %constant_dynamic-update-slice_fusion.1 = bf16[16,3072]{1,0:T(8,128)(2,1)S(1)} fusion(bf16[8,3072]{1,0:T(8,128)(2,1)} %param.10), kind=kLoop, calls=%fused_computation.7 | loop fusion | bytes 98304
  6.4 0.8 %constant_dynamic-update-slice_fusion.3 = bf16[16,3072]{1,0:T(8,128)(2,1)S(1)} fusion(bf16[8,3072]{1,0:T(8,128)(2,1)} %param.11), kind=kLoop, calls=%fused_computation.9 | loop fusion | bytes 98304
  8.5 0.0 collective-permute-done
  8.5 2.2 %collective-permute-start.1 = (bf16[16,3072]{1,0:T(8,128)(2,1)S(1)}, bf16[16,3072]{1,0:T(8,128)(2,1)S(1)}, u32[]{:S(2)}, u32[]{:S(2)}) collective-permute-start(bf16[16,3072]{1,0:T(8,128)(2,1)S(1)} %constant_dynamic-update-slice_fusion.refs_6_.refs_0_), channel_id=1, source_target_pairs={{0,4},{2,6},{4,0},{6,2},{8,12},{10,14},{12,8},{14,10},{1,5},{3,7},... | collective-permute-start | bytes 294920 | tf_op jit(solution)/shard_map/ppermute | solution.py:404
  10.7 1.4 %collective-permute-start.2 = (bf16[16,3072]{1,0:T(8,128)(2,1)S(1)}, bf16[16,3072]{1,0:T(8,128)(2,1)S(1)}, u32[]{:S(2)}, u32[]{:S(2)}) collective-permute-start(bf16[16,3072]{1,0:T(8,128)(2,1)S(1)} %constant_dynamic-update-slice_fusion.refs_6_.refs_0_), channel_id=1, source_target_pairs={{0,6},{2,4},{4,2},{6,0},{8,14},{10,12},{12,10},{14,8},{1,7},{3,5},... | collective-permute-start | bytes 294920 | tf_op jit(solution)/shard_map/ppermute | solution.py:404
  12.1 0.2 collective-permute-start.3
  12.3 0.0 collective-permute-done.5
  12.3 2.0 %collective-permute-start.6 = (bf16[16,3072]{1,0:T(8,128)(2,1)S(1)}, bf16[16,3072]{1,0:T(8,128)(2,1)S(1)}, u32[]{:S(2)}, u32[]{:S(2)}) collective-permute-start(bf16[16,3072]{1,0:T(8,128)(2,1)S(1)} %constant_dynamic-update-slice_fusion.2.refs_0_), channel_id=1, source_target_pairs={{0,4},{2,6},{4,0},{6,2},{8,12},{10,14},{12,8},{14,10},{1,5},{3,7},... | collective-permute-start | bytes 294920 | tf_op jit(solution)/shard_map/ppermute | solution.py:404
  14.3 1.4 %collective-permute-start.7 = (bf16[16,3072]{1,0:T(8,128)(2,1)S(1)}, bf16[16,3072]{1,0:T(8,128)(2,1)S(1)}, u32[]{:S(2)}, u32[]{:S(2)}) collective-permute-start(bf16[16,3072]{1,0:T(8,128)(2,1)S(1)} %constant_dynamic-update-slice_fusion.2.refs_0_), channel_id=1, source_target_pairs={{0,6},{2,4},{4,2},{6,0},{8,14},{10,12},{12,10},{14,8},{1,7},{3,5},... | collective-permute-start | bytes 294920 | tf_op jit(solution)/shard_map/ppermute | solution.py:404
  15.7 1.5 %slot_maps.1 = (s32[1,576]{1,0:T(1,128)S(1)}, s32[1,576]{1,0:T(1,128)S(1)}) custom-call(s32[1,1,576]{2,1,0:T(1,128)} %refs_0_.1, s32[1,1,576]{2,1,0:T(1,128)} %refs_1_.1, s32[1,1,576]{2,1,0:T(1,128)} %refs_2_.1, s32[1,1,576]{2,1,0:T(1,128)} %refs_3_.1, s32[1,1]{1,0:T(1,128)S(6)} %copy.22.refs_4_, s32[1,1]{1,0:T(1,128)S(6)} %copy.23.refs_5_, ...), custom_call_target="tpu_custom_call" | custom-call | bytes 4194304 | tf_op jit(solution)/shard_map/slot_maps/pallas_call | solution.py:63
  17.2 0.0 collective-permute-done.1.refs_1_
  17.2 0.2 collective-permute-start.8
  17.4 0.5 collective-permute-done.2.refs_2_
  17.9 0.0 collective-permute-done.3.refs_3_
  17.9 7.8 %hidden.1 = (bf16[64,3072]{1,0:T(8,128)(2,1)S(1)}, f32[64,3072]{1,0:T(8,128)S(1)}, bf16[64,3072]{1,0:T(8,128)(2,1)S(1)}) custom-call(s32[1,576]{1,0:T(1,128)S(1)} %get-tuple-element.27.slots.refs_5_.refs_3_.refs_0_, bf16[16,3072]{1,0:T(8,128)(2,1)S(1)} %constant_dynamic-update-slice_fusion.refs_6_.refs_0_, ...), custom_call_target="tpu_custom_call" | custom-call | flops 1207959552 | bytes 18874368 | tf_op jit(solution)/shard_map/hidden/pallas_call | solution.py:196
  25.7 0.1 collective-permute-start.4
  25.8 0.0 slice-start
  25.8 0.0 slice-start.1
  25.8 0.0 slice-start.2
  25.8 7.0 %grad_act.1 = (bf16[64,3072]{1,0:T(8,128)(2,1)S(1)}, f32[64,3072]{1,0:T(8,128)S(1)}, bf16[64,3072]{1,0:T(8,128)(2,1)S(1)}) custom-call(s32[1,576]{1,0:T(1,128)S(1)} %get-tuple-element.26.slots.refs_0_, bf16[16,3072]{1,0:T(8,128)(2,1)S(1)} %constant_dynamic-update-slice_fusion.2.refs_0_, bf16[16,3072]{1,0:T(8,128)(2,1)S(1)} %collective-permute-done.6.refs_1_, ...), custom_call_target="tpu_custom_call" | custom-call | flops 1207959552 | bytes 18874368 | tf_op jit(solution)/shard_map/grad_act/pallas_call | solution.py:196
  32.9 0.5 collective-permute-start.9
  33.4 5.8 %output.1 = (bf16[64,3072]{1,0:T(8,128)(2,1)S(1)}, bf16[16,3072]{1,0:T(8,128)(2,1)S(1)}, bf16[16,3072]{1,0:T(8,128)(2,1)S(1)}, bf16[16,3072]{1,0:T(8,128)(2,1)S(1)}, bf16[16,3072]{1,0:T(8,128)(2,1)S(1)}) custom-call(s32[1,576]{1,0:T(1,128)S(1)} %get-tuple-element.26.slots.refs_0_, f32[64,3072]{1,0:T(8,128)S(1)} %get-tuple-element.28.refs_5_.own.hid_own, ...), custom_call_target="tpu_custom_call" | custom-call | flops 1207959552 | bytes 18874368 | tf_op jit(solution)/shard_map/output/pallas_call | solution.py:250
  39.3 7.7 %grad_tokens.1 = (bf16[64,3072]{1,0:T(8,128)(2,1)S(1)}, bf16[32,3072]{1,0:T(8,128)(2,1)S(1)}, bf16[32,3072]{1,0:T(8,128)(2,1)S(1)}, bf16[32,3072]{1,0:T(8,128)(2,1)S(1)}, bf16[32,3072]{1,0:T(8,128)(2,1)S(1)}) custom-call(s32[1,576]{1,0:T(1,128)S(1)} %get-tuple-element.27.slots.refs_5_.refs_3_.refs_0_, f32[64,3072]{1,0:T(8,128)S(1)} %get-tuple-element.28.refs_5_.own.hid_own, ...), custom_call_target="tpu_custom_call" | custom-call | flops 1207959552 | bytes 18874368 | tf_op jit(solution)/shard_map/grad_tokens/pallas_call | solution.py:288
  47.0 1.5 %collective-permute-start.12 = (bf16[32,3072]{1,0:T(8,128)(2,1)S(1)}, bf16[32,3072]{1,0:T(8,128)(2,1)S(1)}, u32[]{:S(2)}, u32[]{:S(2)}) collective-permute-start(bf16[32,3072]{1,0:T(8,128)(2,1)S(1)} %get-tuple-element.44), channel_id=1, source_target_pairs={{0,2},{2,0},{4,6},{6,4},{8,10},{10,8},{12,14},{14,12},{1,3},{3,1},... | collective-permute-start | bytes 589832 | tf_op jit(solution)/shard_map/ppermute | solution.py:404
  48.5 2.3 %collective-permute-start.11 = (bf16[32,3072]{1,0:T(8,128)(2,1)S(1)}, bf16[32,3072]{1,0:T(8,128)(2,1)S(1)}, u32[]{:S(2)}, u32[]{:S(2)}) collective-permute-start(bf16[32,3072]{1,0:T(8,128)(2,1)S(1)} %get-tuple-element.43), channel_id=1, source_target_pairs={{0,6},{2,4},{4,2},{6,0},{8,14},{10,12},{12,10},{14,8},{1,7},{3,5},... | collective-permute-start | bytes 589832 | tf_op jit(solution)/shard_map/ppermute | solution.py:404
  50.8 9.7 %outward.1 = (bf16[576,128,128]{2,1,0:T(8,128)(2,1)}, bf16[576,128,128]{2,1,0:T(8,128)(2,1)}, bf16[32,3072]{1,0:T(8,128)(2,1)S(1)}) custom-call(s32[1,576]{1,0:T(1,128)S(1)} %get-tuple-element.26.slots.refs_0_, bf16[64,3072]{1,0:T(8,128)(2,1)S(1)} %get-tuple-element.31.refs_1_, ...), custom_call_target="tpu_custom_call", output_to_operand_aliasing={{2}: (6, {})} | custom-call | bytes 25165824 | tf_op jit(solution)/shard_map/outward/pallas_call | solution.py:382
  60.5 0.1 fusion.2
  60.7 2.5 %collective-permute-start.13 = (bf16[16,3072]{1,0:T(8,128)(2,1)S(1)}, bf16[16,3072]{1,0:T(8,128)(2,1)S(1)}, u32[]{:S(2)}, u32[]{:S(2)}) collective-permute-start(bf16[16,3072]{1,0:T(8,128)(2,1)S(1)} %pad_maximum_fusion), channel_id=1, source_target_pairs={{0,8},{2,10},{4,12},{6,14},{8,0},{10,2},{12,4},{14,6},{1,9},{3,11}... | collective-permute-start | bytes 294920 | tf_op jit(solution)/shard_map/ppermute | solution.py:404
  63.1 5.5 %inward.1 = (bf16[576,128,128]{2,1,0:T(8,128)(2,1)}, f32[8,128]{1,0:T(8,128)S(1)}) custom-call(s32[1,576]{1,0:T(1,128)S(1)} %get-tuple-element.27.slots.refs_5_.refs_3_.refs_0_, bf16[64,3072]{1,0:T(8,128)(2,1)S(1)} %get-tuple-element.33.refs_4_.refs_1_, ...), custom_call_target="tpu_custom_call", output_to_operand_aliasing={{1}: (3, {}), {0}: (4, {})} | custom-call | bytes 12582912 | tf_op jit(solution)/shard_map/inward/pallas_call | solution.py:382
  68.7 0.7 fusion
  (26 shorter events, 0.1 us)
Async XLA Ops:
  0.6 25.2 %copy-start = (bf16[1,1,576,128,128]{4,3,2,1,0:T(8,128)(2,1)S(1)}, bf16[1,1,576,128,128]{4,3,2,1,0:T(8,128)(2,1)}, u32[]{:S(2)}) copy-start(bf16[1,1,576,128,128]{4,3,2,1,0:T(8,128)(2,1)} %param.16) | copy-start | bytes 56623108
  0.6 7.8 %collective-permute-start = (bf16[8,3072]{1,0:T(8,128)(2,1)}, bf16[8,3072]{1,0:T(8,128)(2,1)S(1)}, u32[]{:S(2)}, u32[]{:S(2)}) collective-permute-start(bf16[8,3072]{1,0:T(8,128)(2,1)} %param.10), channel_id=1, source_target_pairs={{0,8},{2,10},{4,12},{6,14},{8,0},{10,2},{12,4},{14,6},{1,9},{3,11}... | collective-permute-start | bytes 147464 | tf_op jit(solution)/shard_map/ppermute | solution.py:404
  4.7 7.5 %collective-permute-start.5 = (bf16[8,3072]{1,0:T(8,128)(2,1)}, bf16[8,3072]{1,0:T(8,128)(2,1)S(1)}, u32[]{:S(2)}, u32[]{:S(2)}) collective-permute-start(bf16[8,3072]{1,0:T(8,128)(2,1)} %param.11), channel_id=1, source_target_pairs={{0,8},{2,10},{4,12},{6,14},{8,0},{10,2},{12,4},{14,6},{1,9},{3,11}... | collective-permute-start | bytes 147464 | tf_op jit(solution)/shard_map/ppermute | solution.py:404
  8.5 8.7 %collective-permute-start.1 = (bf16[16,3072]{1,0:T(8,128)(2,1)S(1)}, bf16[16,3072]{1,0:T(8,128)(2,1)S(1)}, u32[]{:S(2)}, u32[]{:S(2)}) collective-permute-start(bf16[16,3072]{1,0:T(8,128)(2,1)S(1)} %constant_dynamic-update-slice_fusion.refs_6_.refs_0_), channel_id=1, source_target_pairs={{0,4},{2,6},{4,0},{6,2},{8,12},{10,14},{12,8},{14,10},{1,5},{3,7},... | collective-permute-start | bytes 294920 | tf_op jit(solution)/shard_map/ppermute | solution.py:404
  10.7 7.2 %collective-permute-start.2 = (bf16[16,3072]{1,0:T(8,128)(2,1)S(1)}, bf16[16,3072]{1,0:T(8,128)(2,1)S(1)}, u32[]{:S(2)}, u32[]{:S(2)}) collective-permute-start(bf16[16,3072]{1,0:T(8,128)(2,1)S(1)} %constant_dynamic-update-slice_fusion.refs_6_.refs_0_), channel_id=1, source_target_pairs={{0,6},{2,4},{4,2},{6,0},{8,14},{10,12},{12,10},{14,8},{1,7},{3,5},... | collective-permute-start | bytes 294920 | tf_op jit(solution)/shard_map/ppermute | solution.py:404
  12.1 5.8 %collective-permute-start.3 = (bf16[16,3072]{1,0:T(8,128)(2,1)S(1)}, bf16[16,3072]{1,0:T(8,128)(2,1)S(1)}, u32[]{:S(2)}, u32[]{:S(2)}) collective-permute-start(bf16[16,3072]{1,0:T(8,128)(2,1)S(1)} %constant_dynamic-update-slice_fusion.refs_6_.refs_0_), channel_id=1, source_target_pairs={{0,2},{2,0},{4,6},{6,4},{8,10},{10,8},{12,14},{14,12},{1,3},{3,1},... | collective-permute-start | bytes 294920 | tf_op jit(solution)/shard_map/ppermute | solution.py:404
  12.3 13.5 %collective-permute-start.6 = (bf16[16,3072]{1,0:T(8,128)(2,1)S(1)}, bf16[16,3072]{1,0:T(8,128)(2,1)S(1)}, u32[]{:S(2)}, u32[]{:S(2)}) collective-permute-start(bf16[16,3072]{1,0:T(8,128)(2,1)S(1)} %constant_dynamic-update-slice_fusion.2.refs_0_), channel_id=1, source_target_pairs={{0,4},{2,6},{4,0},{6,2},{8,12},{10,14},{12,8},{14,10},{1,5},{3,7},... | collective-permute-start | bytes 294920 | tf_op jit(solution)/shard_map/ppermute | solution.py:404
  14.3 11.5 %collective-permute-start.7 = (bf16[16,3072]{1,0:T(8,128)(2,1)S(1)}, bf16[16,3072]{1,0:T(8,128)(2,1)S(1)}, u32[]{:S(2)}, u32[]{:S(2)}) collective-permute-start(bf16[16,3072]{1,0:T(8,128)(2,1)S(1)} %constant_dynamic-update-slice_fusion.2.refs_0_), channel_id=1, source_target_pairs={{0,6},{2,4},{4,2},{6,0},{8,14},{10,12},{12,10},{14,8},{1,7},{3,5},... | collective-permute-start | bytes 294920 | tf_op jit(solution)/shard_map/ppermute | solution.py:404
  17.2 8.6 %collective-permute-start.8 = (bf16[16,3072]{1,0:T(8,128)(2,1)S(1)}, bf16[16,3072]{1,0:T(8,128)(2,1)S(1)}, u32[]{:S(2)}, u32[]{:S(2)}) collective-permute-start(bf16[16,3072]{1,0:T(8,128)(2,1)S(1)} %constant_dynamic-update-slice_fusion.2.refs_0_), channel_id=1, source_target_pairs={{0,2},{2,0},{4,6},{6,4},{8,10},{10,8},{12,14},{14,12},{1,3},{3,1},... | collective-permute-start | bytes 294920 | tf_op jit(solution)/shard_map/ppermute | solution.py:404
  25.7 7.7 %collective-permute-start.4 = (bf16[64,3072]{1,0:T(8,128)(2,1)S(1)}, bf16[64,3072]{1,0:T(8,128)(2,1)S(1)}, u32[]{:S(2)}, u32[]{:S(2)}) collective-permute-start(bf16[64,3072]{1,0:T(8,128)(2,1)S(1)} %get-tuple-element.29), channel_id=1, source_target_pairs={{0,1},{1,0},{2,3},{3,2},{4,5},{5,4},{6,7},{7,6},{8,9},{9,8},{10,11... | collective-permute-start | bytes 1179656 | tf_op jit(solution)/shard_map/ppermute | solution.py:438
  25.8 13.5 %slice-start = ((s8[18874368]{0:T(1024)(128)(4,1)}), s8[4194304]{0:T(1024)(128)(4,1)S(1)}, s32[]{:S(2)}) async-start(s8[18874368]{0:T(1024)(128)(4,1)} %bitcast.7), calls=%async_computation | async-start | bytes 8388608
  25.8 13.4 %slice-start.1 = ((s8[18874368]{0:T(1024)(128)(4,1)}), s8[4194304]{0:T(1024)(128)(4,1)S(1)}, s32[]{:S(2)}) async-start(s8[18874368]{0:T(1024)(128)(4,1)} %bitcast.7), calls=%async_computation.1 | async-start | bytes 8388608
  25.8 13.4 %slice-start.2 = ((s8[18874368]{0:T(1024)(128)(4,1)}), s8[4194304]{0:T(1024)(128)(4,1)S(1)}, s32[]{:S(2)}) async-start(s8[18874368]{0:T(1024)(128)(4,1)} %bitcast.7), calls=%async_computation.2 | async-start | bytes 8388608
  32.9 6.4 %collective-permute-start.9 = (bf16[64,3072]{1,0:T(8,128)(2,1)S(1)}, bf16[64,3072]{1,0:T(8,128)(2,1)S(1)}, u32[]{:S(2)}, u32[]{:S(2)}) collective-permute-start(bf16[64,3072]{1,0:T(8,128)(2,1)S(1)} %get-tuple-element.34), channel_id=1, source_target_pairs={{0,1},{1,0},{2,3},{3,2},{4,5},{5,4},{6,7},{7,6},{8,9},{9,8},{10,11... | collective-permute-start | bytes 1179656 | tf_op jit(solution)/shard_map/ppermute | solution.py:438
  33.4 5.9 %slice-start.3 = ((s8[18874368]{0:T(1024)(128)(4,1)}), s8[4194304]{0:T(1024)(128)(4,1)S(1)}, s32[]{:S(2)}) async-start(s8[18874368]{0:T(1024)(128)(4,1)} %bitcast.7), calls=%async_computation.3 | async-start | bytes 8388608
  33.4 5.9 %slice-start.4 = ((s8[18874368]{0:T(1024)(128)(4,1)}), s8[2097152]{0:T(1024)(128)(4,1)S(1)}, s32[]{:S(2)}) async-start(s8[18874368]{0:T(1024)(128)(4,1)} %bitcast.7), calls=%async_computation.4 | async-start | bytes 4194304
  47.0 13.5 %collective-permute-start.12 = (bf16[32,3072]{1,0:T(8,128)(2,1)S(1)}, bf16[32,3072]{1,0:T(8,128)(2,1)S(1)}, u32[]{:S(2)}, u32[]{:S(2)}) collective-permute-start(bf16[32,3072]{1,0:T(8,128)(2,1)S(1)} %get-tuple-element.44), channel_id=1, source_target_pairs={{0,2},{2,0},{4,6},{6,4},{8,10},{10,8},{12,14},{14,12},{1,3},{3,1},... | collective-permute-start | bytes 589832 | tf_op jit(solution)/shard_map/ppermute | solution.py:404
  48.5 12.0 %collective-permute-start.11 = (bf16[32,3072]{1,0:T(8,128)(2,1)S(1)}, bf16[32,3072]{1,0:T(8,128)(2,1)S(1)}, u32[]{:S(2)}, u32[]{:S(2)}) collective-permute-start(bf16[32,3072]{1,0:T(8,128)(2,1)S(1)} %get-tuple-element.43), channel_id=1, source_target_pairs={{0,6},{2,4},{4,2},{6,0},{8,14},{10,12},{12,10},{14,8},{1,7},{3,5},... | collective-permute-start | bytes 589832 | tf_op jit(solution)/shard_map/ppermute | solution.py:404
  50.8 9.7 %collective-permute-start.10 = (bf16[32,3072]{1,0:T(8,128)(2,1)S(1)}, bf16[32,3072]{1,0:T(8,128)(2,1)S(1)}, u32[]{:S(2)}, u32[]{:S(2)}) collective-permute-start(bf16[32,3072]{1,0:T(8,128)(2,1)S(1)} %get-tuple-element.42), channel_id=1, source_target_pairs={{0,4},{2,6},{4,0},{6,2},{8,12},{10,14},{12,8},{14,10},{1,5},{3,7},... | collective-permute-start | bytes 589832 | tf_op jit(solution)/shard_map/ppermute | solution.py:404
  60.7 8.0 %collective-permute-start.13 = (bf16[16,3072]{1,0:T(8,128)(2,1)S(1)}, bf16[16,3072]{1,0:T(8,128)(2,1)S(1)}, u32[]{:S(2)}, u32[]{:S(2)}) collective-permute-start(bf16[16,3072]{1,0:T(8,128)(2,1)S(1)} %pad_maximum_fusion), channel_id=1, source_target_pairs={{0,8},{2,10},{4,12},{6,14},{8,0},{10,2},{12,4},{14,6},{1,9},{3,11}... | collective-permute-start | bytes 294920 | tf_op jit(solution)/shard_map/ppermute | solution.py:404
